TPU v7x, 256 devices: a whole 4x4x8 slice. The times are simulated.
256 devices in a mesh: wide: 32 (over z, y_lo, core), narrow: 8 (over y_hi, x).
Axes of the slice: x: 4, y: 4 (y_hi: 2, y_lo: 2; y = y_hi * 2 + y_lo), z: 8, core: 2. Of those that a mesh axis runs over, the one named last changes fastest.
Arguments:
- tokens: bfloat16 [3072, 8192], P('wide', 'narrow')
- grad_out: bfloat16 [3072, 8192], P('wide', 'narrow'), may hold values from -6 to 6
- selected: int32 [384], replicated, may hold values from 0 to 3071, as said below
- gain: float32 [8192], P('narrow'), may hold values from 0.1 to 1.9
- router_weight: float32 [8192], P('narrow'), may hold values from -0.0625 to 0.0625
- w_gate: bfloat16 [8192, 32768], P('narrow', 'wide'), may hold values from -0.0625 to 0.0625
- w_up: bfloat16 [8192, 32768], P('narrow', 'wide'), may hold values from -0.0625 to 0.0625
- w_down: bfloat16 [32768, 8192], P('wide', 'narrow'), may hold values from -0.03125 to 0.03125
Outputs:
- grad_x: bfloat16 [3072, 8192], P('wide', 'narrow')
- grad_gate: bfloat16 [8192, 32768], P('narrow', 'wide')
- grad_up: bfloat16 [8192, 32768], P('narrow', 'wide')
- grad_down: bfloat16 [32768, 8192], P('wide', 'narrow')
- grad_gain: float32 [8192], P('narrow')
- grad_router: float32 [8192], P('narrow')
Inputs may be any that keep to these rules, and one draw needn't show every extreme that they name: The ids rise strictly. Each aligned block of 96 token ids holds at most 24 selected ids, and some block holds exactly 24.
All inputs are finite; a program needn't handle non-finite values.
Results may differ from a plain program's by a relative error of at most 0.008.
Values may be sent and summed in bfloat16 or wider, within the bound.
No kernel may reach another device: no remote copies, remote signals or barrier semaphores. Data moves between devices by JAX's collectives and lax.ppermute only.
A program may use at most 128 MiB of HBM per device.

v0:
```python
import jax
import jax.numpy as jnp
from jax import lax
from jax.experimental import pallas as pl
from jax.experimental.pallas import tpu as pltpu
from jax.sharding import PartitionSpec as P

D = 8192
EPS = 1e-06
bf16 = jnp.bfloat16
f32 = jnp.float32
i32 = jnp.int32
DOWN, UP = 2.0**-20, 2.0**20
TOK = 96
CAP = 24
SEL = 384
W = 1024
TILE = 256
WIDER = 512

WIDE = [(z, y, c) for z in range(8) for y in range(2) for c in range(2)]


def wide_pairs(move):
    def index(z, y, c):
        return (z % 8 * 2 + y) * 2 + c

    return [(index(*t), index(*move(*t))) for t in WIDE]


CORE = wide_pairs(lambda z, y, c: (z, y, 1 - c))
YLO = wide_pairs(lambda z, y, c: (z, 1 - y, c))
XUP = [(n, n // 4 * 4 + (n + 1) % 4) for n in range(8)]
XDOWN = [(n, n // 4 * 4 + (n + 3) % 4) for n in range(8)]
XFAR = [(n, n // 4 * 4 + (n + 2) % 4) for n in range(8)]
YHI = [(n, (n + 4) % 8) for n in range(8)]
ROW = 3 * 1024 + 128
ZFAR = wide_pairs(lambda z, y, c: (z + 2 + 4 * c, y, c))


def along(value, step):
    return lax.ppermute(value, "wide", wide_pairs(lambda z, y, c: (z + 8 + step, y, c)))


VMEM = pl.BlockSpec(memory_space=pltpu.VMEM)


def params(mib=24):
    return pltpu.CompilerParams(vmem_limit_bytes=mib << 20)


def cost(flops, bytes_):
    return pl.CostEstimate(flops=int(flops), bytes_accessed=int(bytes_), transcendentals=0)


def heads(value, count):
    out = []
    for _ in range(count):
        head = value.astype(bf16).astype(f32)
        out.append(head)
        value = jnp.where(jnp.abs(head) < jnp.inf, value - head, 0.0)
    return out


def lanes_of(columns, rows):
    lane = lax.broadcasted_iota(i32, (rows, 128), 1)
    out = jnp.zeros((rows, 128), f32)
    for k, column in enumerate(columns):
        out = jnp.where(lane == k, column, out)
    return out.astype(bf16)


def span(i, size, start=0):
    return pl.ds(pl.multiple_of(start + i * size, size), size)


def mm(a, b, ca, cb):
    return lax.dot_general(a, b, (((ca,), (cb,)), ((), ())), preferred_element_type=f32)


def place_of():
    w = lax.axis_index("wide")
    return w, w // 4, (w // 2) % 2, w % 2


def count_before(sel_col, ids):
    return jnp.sum(jnp.where(sel_col < ids, 1, 0).astype(i32), axis=0, keepdims=True)


def compact_of(i):
    n = lax.axis_index("narrow")
    r = (i * 1366) >> 16
    block = (r & 4 ^ n & 4) | ((r + n) & 3)
    return i + (block - r) * 48


def placement(sel_col, begin, size):
    _, z, y, c = place_of()
    slot = begin + lax.broadcasted_iota(i32, (1, size), 1)
    n = (slot * 2731) >> 16
    k = slot - n * CAP
    zz = (z + ((n >> 1) & 7) + 5) & 7
    block = zz * 4 + (y ^ (n & 1)) * 2 + (c ^ (n >> 4))
    start = count_before(sel_col, block * TOK)
    end = count_before(sel_col, block * TOK + TOK)
    row = compact_of(lax.broadcasted_iota(i32, (SEL, 1), 0))
    return jnp.where((row == start + k) & (row < end), 1.0, 0.0)


def pick_of(sel_row):
    w, _, _, _ = place_of()

    def before(ids):
        return jnp.sum(jnp.where(sel_row < ids, 1, 0).astype(i32), axis=1, keepdims=True)

    ids = w * TOK + lax.broadcasted_iota(i32, (TOK, 1), 0)
    first = before(jnp.full((1, 1), w * TOK, i32))
    last = before(jnp.full((1, 1), w * TOK + TOK, i32))
    rank = before(ids) - first
    marked = before(ids + 1) - before(ids) > 0
    k = lax.broadcasted_iota(i32, (TOK, CAP), 1)
    return jnp.where((k == rank) & marked, 1.0, 0.0).astype(bf16), first, last


def own_kernel(sel_hbm, tok_hbm, go_hbm, out, row, sel, tok, go, sems):
    copies = [
        pltpu.make_async_copy(tok_hbm, tok, sems.at[0]),
        pltpu.make_async_copy(go_hbm, go, sems.at[1]),
        pltpu.make_async_copy(sel_hbm, sel, sems.at[2]),
    ]
    for copy in copies:
        copy.start()
    copies[2].wait()
    sel_row = sel[...].reshape(1, SEL)
    row[...] = sel_row
    pick = pick_of(sel_row)[0]
    for n, held in enumerate((tok, go)):
        copies[n].wait()
        out[:, n * W : n * W + W] = mm(pick, held[...], 0, 0).astype(bf16)


def onehot_kernel(sel_col, gain, rw, _, *refs):
    weights, (put, spread, vectors), held, sems = refs[:3], refs[3:6], refs[6:9], refs[9]
    loads = [pltpu.make_async_copy(weights[n], held[n], sems.at[n]) for n in range(3)]
    for load in loads:
        load.start()
    vectors[0:1, :] = gain[...]
    vectors[1:2, :] = rw[...]
    @pl.loop(0, 2 * SEL // 128)
    def _(i):
        hot = placement(sel_col[...], i * 128, 128)
        put[:, span(i, 128)] = hot.astype(bf16)
        spread[span(i, 128), :] = hot.T.astype(bf16)

    for load in loads:
        load.wait()


def forward_kernel(*refs):
    parts = refs[:16]
    put, vectors, *held, sel, gsel, keep = refs[16:24]
    to_up, to_down, to_y, near_up, near_down, slots, scaled = refs[24:]

    def write(lo, hi, value):
        value = value.astype(bf16)
        for r, (out, at) in enumerate(
            (
                (keep, 0),
                (near_up, 0),
                (keep, 96),
                (near_down, 0),
                (keep, 48),
                (to_up, 0),
                (to_y, 0),
                (to_down, 0),
            )
        ):
            out[at : at + 48, lo:hi] = value[48 * r : 48 * r + 48]

    for p in range(16):
        slots[48 * p : 48 * p + 48, :] = parts[p][...]
    squares = jnp.zeros((SEL, 128), f32)
    logit = jnp.zeros((SEL, 128), f32)
    for lo in range(0, W, WIDER):
        hi = lo + WIDER
        tile = mm(put[...], slots[:, lo:hi], 1, 0)
        sel[:, lo:hi] = tile.astype(bf16)
        for m in range(0, WIDER, 128):
            lanes = tile[:, m : m + 128]
            squares += lanes * lanes
            logit += lanes * vectors[1:2, lo + m : lo + m + 128]
        scaled[:, lo:hi] = (tile * (vectors[0:1, lo:hi] * DOWN)).astype(bf16)
    squares = jnp.sum(squares, axis=1, keepdims=True)
    logit = jnp.sum(logit, axis=1, keepdims=True)
    write(3 * W, ROW, lanes_of(heads(squares, 3) + heads(logit, 3), SEL))
    for n in range(2):
        for lo in range(0, W, WIDER):
            write(n * W + lo, n * W + lo + WIDER, mm(scaled[...], held[n][:, lo : lo + WIDER], 1, 0))
    for lo in range(W, 2 * W, WIDER):
        gsel[:, lo - W : lo - W + WIDER] = mm(put[...], slots[:, lo : lo + WIDER], 1, 0).astype(
            bf16
        )
    for lo in range(0, W, WIDER):
        write(2 * W + lo, 2 * W + lo + WIDER, mm(gsel[...], held[2][lo : lo + WIDER, :], 1, 1))


def stats(refs):
    tail = 0.0
    for ref in refs:
        tail = tail + ref[:, 3 * W :].astype(f32)
    return (
        tail[:, 0:1] + tail[:, 1:2] + tail[:, 2:3],
        tail[:, 3:4] + tail[:, 4:5] + tail[:, 5:6],
    )


def sum_kernel(keep, from_below, from_above, from_y, to_y, to_far):
    for out, refs in (
        (to_y, (keep.at[48:96], from_below, from_above)),
        (to_far, (keep.at[96:144], from_y)),
    ):

        @pl.loop(0, 3 * W // TILE)
        def _(k, out=out, refs=refs):
            cols = span(k, TILE)
            total = refs[0][:, cols].astype(f32)
            for ref in refs[1:]:
                total = total + ref[:, cols].astype(f32)
            out[:, cols] = total.astype(bf16)

        squares, logit = stats(refs)
        out[:, 3 * W :] = lanes_of(heads(squares, 3) + heads(logit, 3), SEL // 8)


def hidden_kernel(keep, near_below, near_above, from_y, from_far, out):
    rows = SEL // 8
    refs = (keep.at[0:48], near_below, near_above, from_y, from_far)

    squares, logit = stats(refs)
    scale = lax.rsqrt(squares / D + EPS)

    def tile(i, carry):
        router_grad, inner = carry

        def total(start):
            cols = span(i, TILE, start)
            value = refs[0][:, cols].astype(f32)
            for ref in refs[1:]:
                value = value + ref[:, cols].astype(f32)
            return value

        gate = total(0) * (scale * UP)
        upv = total(W) * (scale * UP)
        back = total(2 * W)
        sigma = jax.nn.sigmoid(gate)
        hidden = (gate * sigma * upv).astype(bf16)
        d_hidden = logit * back
        d_gate = (d_hidden * upv * (sigma + gate * sigma * (1.0 - sigma))).astype(bf16)
        d_up = (d_hidden * gate * sigma).astype(bf16)
        router_grad += jnp.sum(hidden.astype(f32) * back, axis=1, keepdims=True)
        inner += jnp.sum(
            d_gate.astype(f32) * gate + d_up.astype(f32) * upv, axis=1, keepdims=True
        )
        out[:, span(i, TILE)] = d_gate
        out[:, span(i, TILE, W)] = d_up
        out[:, span(i, TILE, 2 * W)] = hidden
        return router_grad, inner

    zero = jnp.zeros((rows, 1), f32)
    router_grad, inner = lax.fori_loop(0, W // TILE, tile, (zero, zero))
    out[:, 3 * W :] = lanes_of(
        heads(scale, 3) + heads(logit, 3) + heads(router_grad, 3) + heads(inner, 3), rows
    )


def with_small(rows, small):
    return jnp.concatenate([rows] + heads(small, 2), axis=0).astype(bf16)


def apart(ref, cols):
    value = ref[:, cols].astype(f32)
    n = value.shape[0] - 8
    return value[:n], value[n : n + 4] + value[n + 4 : n + 8]


def to_row(column):
    eye = lax.broadcasted_iota(i32, (SEL, SEL), 0) == lax.broadcasted_iota(i32, (SEL, SEL), 1)
    return jnp.sum(jnp.where(eye, column, 0.0), axis=0, keepdims=True)


def normed_kernel(
    spread, own, above, b2, below, b4, b6, wg, wu, sel, theirs, ours, small, gd, cols
):
    j = pl.program_id(0)

    @pl.when(j == 0)
    def _():
        tail = []
        for r, (ref, at) in enumerate(
            (
                (own, 0),
                (above, 0),
                (b2, 0),
                (below, 0),
                (b4, 0),
                (above, 48),
                (b6, 0),
                (below, 48),
            )
        ):
            gd[48 * r : 48 * r + 48, :] = ref[at : at + 48, 0 : 2 * W]
            tail.append(ref[at : at + 48, 3 * W :].astype(f32))
        tail = jnp.concatenate(tail, axis=0)
        lane = lax.broadcasted_iota(i32, (SEL, 128), 1)

        def value(k):
            return jnp.sum(
                jnp.where((lane >= 3 * k) & (lane < 3 * k + 3), tail, 0.0), axis=1, keepdims=True
            )

        scale, router_grad, inner = value(0), value(2), value(3)
        cols[...] = jnp.where(lane == 0, scale, router_grad)
        small[...] = jnp.zeros(small.shape, f32)
        small[2:3, 0:SEL] = to_row(router_grad)
        small[2:3, SEL : 2 * SEL] = to_row(inner)
        small[3:4, 0:SEL] = to_row(scale)

    part = mm(gd[:, 0:W], wg[...], 1, 1) + mm(gd[:, W : 2 * W], wu[...], 1, 1)
    sel32 = sel[...].astype(f32)
    at = pl.ds(pl.multiple_of(j * W, W), W)
    small[0:1, at] = jnp.sum(part * sel32 * cols[:, 0:1], axis=0, keepdims=True)
    small[1:2, at] = jnp.sum(sel32 * cols[:, 1:2], axis=0, keepdims=True)
    rounded = part.astype(bf16)
    ours[...] = mm(spread[:SEL, :], rounded, 1, 0).astype(bf16)
    theirs[...] = with_small(mm(spread[SEL:, :], rounded, 1, 0), small[0:4, at])


def join_kernel(ours, theirs, mine, up3, down3, far, up1, down1, small):
    @pl.loop(0, W // TILE)
    def _(i):
        cols = span(i, TILE)
        rows, other = apart(theirs, cols)
        total = mine[0:4, cols] + other
        small[:, cols] = total
        for n, out in ((0, down3), (2, down1), (4, up1), (6, up3), (7, far)):
            at = slice(48 * n, 48 * n + 48)
            out[:, cols] = with_small(ours[at, cols].astype(f32) + rows[at], total)


def relay_kernel(
    up2, up2_other, from_below, down2, down2_other, from_above, far, small, to_up, to_down
):
    _, _, _, c = place_of()

    @pl.loop(0, W // TILE)
    def _(i):
        cols = span(i, TILE)
        rows, one = apart(far, cols)
        for base, other, ref, mask, out in (
            (up2, up2_other, from_below, c == 0, to_up),
            (down2, down2_other, from_above, c == 1, to_down),
        ):
            chunk, two = apart(ref, cols)
            chunk += base[:, cols].astype(f32) + other[:, cols].astype(f32)
            out[:, cols] = with_small(
                chunk + jnp.where(mask, rows, 0.0),
                small[:, cols] + two + jnp.where(mask, one, 0.0),
            )


def pair_kernel(stay, stay_other, small, a, b, c, d, here, there):
    @pl.loop(0, W // TILE)
    def _(i):
        cols = span(i, TILE)
        total = stay[:, cols].astype(f32) + stay_other[:, cols].astype(f32)
        low = small[:, cols]
        for part in (a, b, c, d):
            rows, other = apart(part, cols)
            total, low = total + rows, low + other
        here[0:CAP, cols] = total[:CAP]
        here[CAP : CAP + 4, cols] = low
        there[:, cols] = with_small(total[CAP:], low)


def far_kernel(below, above, _, out):
    out[...] = jnp.where(place_of()[3] == 0, below[...], above[...])


def final_kernel(
    here, there, mine, go, vectors, sel_row, small, grad_x, d_gain, d_router, held
):
    pick, first, last = pick_of(sel_row[...])
    own, summed = apart(there, slice(0, W))
    own = own + here[0:CAP, :]
    summed = summed + here[CAP : CAP + 4, :]
    d_gain[...] = summed[0:1]
    d_router[...] = summed[1:2]
    row = compact_of(lax.broadcasted_iota(i32, (1, SEL), 1))
    k = lax.broadcasted_iota(i32, (CAP, SEL), 0)
    where = (row == first + k) & (row < last)

    def place(values):
        return jnp.sum(jnp.where(where, values, 0.0), axis=1, keepdims=True)

    scale = place(small[3:4, 0:SEL])
    router_grad = place(summed[2:3, 0:SEL])
    inner = place(summed[2:3, SEL : 2 * SEL])
    held[...] = own

    @pl.loop(0, W // TILE)
    def _(i):
        cols = span(i, TILE)
        d_sel = (
            scale * vectors[0:1, cols] * held[:, cols]
            - mine[:, cols].astype(f32) * (scale * scale * inner / D)
            + router_grad * vectors[1:2, cols]
        )
        spread = jnp.zeros((TOK, TILE), f32)
        for piece in heads(d_sel, 3):
            spread += mm(pick, piece.astype(bf16), 1, 0)
        grad_x[:, cols] = (go[:, cols].astype(f32) + spread).astype(bf16)


def gather(pair, after):
    held = {0: pair}
    for k in (2, 1):
        held[-k] = along(pair, k)
        held[k] = along(pair, -k)
    held[-3] = along(held[-2], 1)
    held[3] = along(held[2], -1)
    far = pl.pallas_call(
        far_kernel,
        out_shape=jax.ShapeDtypeStruct(pair.shape, bf16),
        in_specs=[VMEM] * 2 + [pl.BlockSpec(memory_space=pl.ANY)],
        out_specs=VMEM,
        compiler_params=params(16),
        name="far",
    )(held[-2], held[2], after)
    held[4] = lax.ppermute(far, "wide", ZFAR)
    ours = [held[k] for k in range(-3, 5)]
    return ours + [lax.ppermute(piece, "wide", CORE) for piece in ours]


def local(tokens, grad_out, selected, gain, router_weight, w_gate, w_up, w_down):
    sel_col = selected.reshape(SEL, 1)
    gain = gain.reshape(1, W)
    router_weight = router_weight.reshape(1, W)
    anywhere = pl.BlockSpec(memory_space=pl.ANY)
    mine, sel_row = pl.pallas_call(
        own_kernel,
        out_shape=(
            jax.ShapeDtypeStruct((CAP, 2 * W), bf16),
            jax.ShapeDtypeStruct((1, SEL), i32),
        ),
        in_specs=[anywhere] * 3,
        out_specs=(VMEM, VMEM),
        scratch_shapes=[pltpu.VMEM((SEL,), i32)]
        + [pltpu.VMEM((TOK, W), bf16)] * 2
        + [pltpu.SemaphoreType.DMA((3,))],
        compiler_params=params(60),
        name="own",
    )(selected, tokens, grad_out)
    put, spread, vectors, *weights = pl.pallas_call(
        onehot_kernel,
        out_shape=(
            jax.ShapeDtypeStruct((SEL, 2 * SEL), bf16),
            jax.ShapeDtypeStruct((2 * SEL, SEL), bf16),
            jax.ShapeDtypeStruct((2, W), f32),
        )
        + (jax.ShapeDtypeStruct((W, W), bf16),) * 3,
        in_specs=[VMEM] * 3 + [anywhere] * 4,
        out_specs=(VMEM,) * 6,
        scratch_shapes=[pltpu.SemaphoreType.DMA((3,))],
        compiler_params=params(16),
        name="onehot",
    )(sel_col, gain, router_weight, mine, w_gate, w_up, w_down)
    pair = jnp.concatenate([mine, lax.ppermute(mine, "wide", YLO)], axis=0)
    parts = gather(pair, put)

    full = lambda *shape: pl.BlockSpec(shape, lambda j: (0,) * len(shape))
    block = jax.ShapeDtypeStruct((48, ROW), bf16)
    sel, gsel, keep, to_up, to_down, to_y, *near = pl.pallas_call(
        forward_kernel,
        out_shape=(
            jax.ShapeDtypeStruct((SEL, W), bf16),
            jax.ShapeDtypeStruct((SEL, W), bf16),
            jax.ShapeDtypeStruct((144, ROW), bf16),
        )
        + (block,) * 5,
        in_specs=[VMEM] * 21,
        out_specs=(VMEM,) * 8,
        scratch_shapes=[pltpu.VMEM((768, 2 * W), bf16), pltpu.VMEM((SEL, W), bf16)],
        compiler_params=params(16),
        cost_estimate=cost(3.6e9, 16e6),
        name="forward",
    )(*parts, put, vectors, *weights)

    from_below = lax.ppermute(to_up, "narrow", XUP)
    from_above = lax.ppermute(to_down, "narrow", XDOWN)
    from_y = lax.ppermute(to_y, "narrow", YHI)
    near = lax.ppermute(near[0], "narrow", XUP), lax.ppermute(near[1], "narrow", XDOWN)
    to_y, to_far = pl.pallas_call(
        sum_kernel,
        out_shape=(block, block),
        in_specs=[VMEM] * 4,
        out_specs=(VMEM, VMEM),
        compiler_params=params(8),
        name="sum",
    )(keep, from_below, from_above, from_y)
    from_far = lax.ppermute(to_far, "narrow", XFAR)
    from_y = lax.ppermute(to_y, "narrow", YHI)
    own = pl.pallas_call(
        hidden_kernel,
        out_shape=block,
        in_specs=[VMEM] * 5,
        out_specs=VMEM,
        compiler_params=params(8),
        name="hidden",
    )(keep, *near, from_y, from_far)

    b2 = lax.ppermute(own, "narrow", XFAR)
    b4 = lax.ppermute(own, "narrow", YHI)
    column = jnp.concatenate([own, b4], axis=0)
    below = lax.ppermute(column, "narrow", XUP)
    above = lax.ppermute(column, "narrow", XDOWN)
    b6 = lax.ppermute(b2, "narrow", YHI)

    theirs, ours, small = pl.pallas_call(
        normed_kernel,
        grid=(W // W,),
        out_shape=(
            jax.ShapeDtypeStruct((SEL + 8, W), bf16),
            jax.ShapeDtypeStruct((SEL, W), bf16),
            jax.ShapeDtypeStruct((8, W), f32),
        ),
        in_specs=[VMEM] * 7
        + [pl.BlockSpec((W, W), lambda j: (j, 0))] * 2
        + [pl.BlockSpec((SEL, W), lambda j: (0, j))],
        out_specs=(
            pl.BlockSpec((SEL + 8, W), lambda j: (0, j)),
            pl.BlockSpec((SEL, W), lambda j: (0, j)),
            full(8, W),
        ),
        scratch_shapes=[pltpu.VMEM((SEL, 2 * W), bf16), pltpu.VMEM((SEL, 128), f32)],
        compiler_params=params(),
        cost_estimate=cost(2.4e9, 9e6),
        name="normed",
    )(spread, own, above, b2, below, b4, b6, w_gate, w_up, sel)

    part = jax.ShapeDtypeStruct((56, W), bf16)
    theirs = lax.ppermute(theirs, "wide", CORE)
    up3, down3, far, up1, down1, total = pl.pallas_call(
        join_kernel,
        out_shape=(part,) * 5 + (jax.ShapeDtypeStruct((4, W), f32),),
        in_specs=[VMEM] * 3,
        out_specs=(VMEM,) * 6,
        compiler_params=params(16),
        name="join",
    )(ours, theirs, small)
    from_below, from_above = along(up3, 1), along(down3, -1)
    far = lax.ppermute(far, "wide", ZFAR)
    near = along(up1, 1), along(down1, -1)

    def chunk(n):
        return pl.BlockSpec((48, W), lambda j: (n, 0))

    up2, down2 = pl.pallas_call(
        relay_kernel,
        grid=(1,),
        out_shape=(part, part),
        in_specs=[chunk(5), chunk(5), full(56, W), chunk(1), chunk(1)]
        + [full(56, W), full(56, W), full(4, W)],
        out_specs=(full(56, W), full(56, W)),
        compiler_params=params(16),
        name="relay",
    )(ours, theirs, from_below, ours, theirs, from_above, far, total)
    here, there = pl.pallas_call(
        pair_kernel,
        grid=(1,),
        out_shape=(
            jax.ShapeDtypeStruct((CAP + 4, W), f32),
            jax.ShapeDtypeStruct((CAP + 8, W), bf16),
        ),
        in_specs=[chunk(3), chunk(3), full(4, W)] + [full(56, W)] * 4,
        out_specs=(full(CAP + 4, W), full(CAP + 8, W)),
        compiler_params=params(16),
        name="pair",
    )(ours, theirs, total, *near, along(up2, 2), along(down2, -2))
    there = lax.ppermute(there, "wide", YLO)

    rows = jnp.concatenate([own, above[:48], b2, below[:48], b4, above[48:], b6, below[48:]])
    tail = rows[:, 3 * W :].astype(f32)
    scale = jnp.sum(tail[:, 0:3], axis=1, keepdims=True)
    logit = jnp.sum(tail[:, 3:6], axis=1, keepdims=True)
    normed = (sel.astype(f32) * scale * gain).astype(bf16)
    d_out = (logit * gsel.astype(f32)).astype(bf16)
    grad_gate = mm(normed, rows[:, :W], 0, 0).astype(bf16)
    grad_up = mm(normed, rows[:, W : 2 * W], 0, 0).astype(bf16)
    grad_down = mm(rows[:, 2 * W : 3 * W], d_out, 0, 0).astype(bf16)

    vector = jax.ShapeDtypeStruct((1, W), f32)
    grad_x, d_gain, d_router = pl.pallas_call(
        final_kernel,
        out_shape=(jax.ShapeDtypeStruct((TOK, W), bf16), vector, vector),
        in_specs=[VMEM] * 7,
        out_specs=(VMEM,) * 3,
        scratch_shapes=[pltpu.VMEM((CAP, W), f32)],
        compiler_params=params(16),
        name="final",
    )(here, there, mine, grad_out, vectors, sel_row, small)
    return (grad_x, grad_gate, grad_up, grad_down, d_gain.reshape(W), d_router.reshape(W))


def solution(mesh):
    return jax.shard_map(
        local,
        mesh=mesh,
        in_specs=(
            P("wide", "narrow"),
            P("wide", "narrow"),
            P(),
            P("narrow"),
            P("narrow"),
            P("narrow", "wide"),
            P("narrow", "wide"),
            P("wide", "narrow"),
        ),
        out_specs=(
            P("wide", "narrow"),
            P("narrow", "wide"),
            P("narrow", "wide"),
            P("wide", "narrow"),
            P("narrow"),
            P("narrow"),
        ),
        check_vma=False,
    )
```

profile of v0, /device:TPU:22, one launch (start us, length us, event | category | flops | bytes accessed | tf_op | source)
XLA Modules:
  0.0 128.7 jit_solution(17466681829756959300)
XLA Ops:
  0.6 2.0 %own.1 = (bf16[24,2048]{1,0:T(8,128)(2,1)}, s32[1,384]{1,0:T(1,128)}) custom-call(s32[384]{0:T(512)} %sel_hbm.1, bf16[96,1024]{1,0:T(8,128)(2,1)} %tok_hbm.1, bf16[96,1024]{1,0:T(8,128)(2,1)} %go.1), custom_call_target="tpu_custom_call" | custom-call | tf_op jit(solution)/shard_map/own/pallas_call | solution.py:449
  5.0 2.6 %collective-permute-done = bf16[24,2048]{1,0:T(8,128)(2,1)S(1)} collective-permute-done((bf16[24,2048]{1,0:T(8,128)(2,1)}, bf16[24,2048]{1,0:T(8,128)(2,1)S(1)}, u32[]{:S(2)}, u32[]{:S(2)}) %collective-permute-start) | collective-permute-done | bytes 98336 | tf_op jit(solution)/shard_map/ppermute | solution.py:477
  7.6 6.4 %collective-permute-start.5 = (bf16[48,2048]{1,0:T(8,128)(2,1)S(1)}, bf16[48,2048]{1,0:T(8,128)(2,1)S(1)}, u32[]{:S(2)}, u32[]{:S(2)}) collective-permute-start(bf16[48,2048]{1,0:T(8,128)(2,1)S(1)} %constant_dynamic-update-slice_fusion.refs_3_), channel_id=1, source_target_pairs={{0,192},{8,200},{16,208},{24,216},{32,224},{40,232},{48,240},{56,2... | collective-permute-start | bytes 589832 | tf_op jit(solution)/shard_map/ppermute | solution.py:42
  24.3 2.1 %onehot.1 = (bf16[384,768]{1,0:T(8,128)(2,1)S(1)}, bf16[768,384]{1,0:T(8,128)(2,1)S(1)}, f32[2,1024]{1,0:T(2,128)S(1)}, bf16[1024,1024]{1,0:T(8,128)(2,1)S(1)}, ...) custom-call(s32[384,1]{1,0:T(8,128)S(1)} %reshape.35.sel_col, f32[1,1024]{1,0:T(1,128)S(1)} %bitcast.5, ...), custom_call_target="tpu_custom_call" | custom-call | tf_op jit(solution)/shard_map/onehot/pallas_call | solution.py:463
  27.0 3.0 %collective-permute-start.6 = (bf16[48,2048]{1,0:T(8,128)(2,1)S(1)}, bf16[48,2048]{1,0:T(8,128)(2,1)S(1)}, u32[]{:S(2)}, u32[]{:S(2)}) collective-permute-start(bf16[48,2048]{1,0:T(8,128)(2,1)S(1)} %collective-permute-done.5.above.refs_5_), channel_id=1, source_target_pairs={{0,224},{8,232},{16,240},{24,248},{32,0},{40,8},{48,16},{56,24},{6... | collective-permute-start | bytes 589832 | tf_op jit(solution)/shard_map/ppermute | solution.py:42
  30.2 2.3 %collective-permute-start.9 = (bf16[48,2048]{1,0:T(8,128)(2,1)S(1)}, bf16[48,2048]{1,0:T(8,128)(2,1)S(1)}, u32[]{:S(2)}, u32[]{:S(2)}) collective-permute-start(bf16[48,2048]{1,0:T(8,128)(2,1)S(1)} %collective-permute-done.1.below.refs_1_), channel_id=1, source_target_pairs={{0,8},{8,0},{16,24},{24,16},{32,40},{40,32},{48,56},{56,48},{64,72... | collective-permute-start | bytes 589832 | tf_op jit(solution)/shard_map/ppermute | solution.py:441
  32.5 3.3 %collective-permute-done.6.refs_6_ = bf16[48,2048]{1,0:T(8,128)(2,1)S(1)} collective-permute-done((bf16[48,2048]{1,0:T(8,128)(2,1)S(1)}, bf16[48,2048]{1,0:T(8,128)(2,1)S(1)}, u32[]{:S(2)}, u32[]{:S(2)}) %collective-permute-start.6) | collective-permute-done | bytes 196640 | tf_op jit(solution)/shard_map/ppermute | solution.py:42
  36.3 4.4 %collective-permute-done.2.refs_0_ = bf16[48,2048]{1,0:T(8,128)(2,1)S(1)} collective-permute-done((bf16[48,2048]{1,0:T(8,128)(2,1)S(1)}, bf16[48,2048]{1,0:T(8,128)(2,1)S(1)}, u32[]{:S(2)}, u32[]{:S(2)}) %collective-permute-start.2) | collective-permute-done | bytes 196640 | tf_op jit(solution)/shard_map/ppermute | solution.py:42
  42.4 4.1 %forward.1 = (bf16[384,1024]{1,0:T(8,128)(2,1)S(1)}, bf16[384,1024]{1,0:T(8,128)(2,1)S(1)}, bf16[144,3200]{1,0:T(8,128)(2,1)S(1)}, bf16[48,3200]{1,0:T(8,128)(2,...) custom-call(bf16[48,2048]{1,0:T(8,128)(2,1)S(1)} %collective-permute, ...), custom_call_target="tpu_custom_call" | custom-call | flops 3600000000 | bytes 16000000 | tf_op jit(solution)/shard_map/forward/pallas_call | solution.py:482
  51.0 5.7 %collective-permute-done.18.from_below = bf16[48,3200]{1,0:T(8,128)(2,1)S(1)} collective-permute-done((bf16[48,3200]{1,0:T(8,128)(2,1)S(1)}, bf16[48,3200]{1,0:T(8,128)(2,1)S(1)}, u32[]{:S(2)}, u32[]{:S(2)}) %collective-permute-start.18) | collective-permute-done | bytes 307232 | tf_op jit(solution)/shard_map/ppermute | solution.py:498
  63.3 7.3 %collective-permute-done.17.near_above = bf16[48,3200]{1,0:T(8,128)(2,1)S(1)} collective-permute-done((bf16[48,3200]{1,0:T(8,128)(2,1)S(1)}, bf16[48,3200]{1,0:T(8,128)(2,1)S(1)}, u32[]{:S(2)}, u32[]{:S(2)}) %collective-permute-start.17) | collective-permute-done | bytes 307232 | tf_op jit(solution)/shard_map/ppermute | solution.py:501
  71.6 1.9 %collective-permute-start.23 = (bf16[48,3200]{1,0:T(8,128)(2,1)S(1)}, bf16[48,3200]{1,0:T(8,128)(2,1)S(1)}, u32[]{:S(2)}, u32[]{:S(2)}) collective-permute-start(bf16[48,3200]{1,0:T(8,128)(2,1)S(1)} %hidden.1.own), channel_id=1, source_target_pairs={{0,4},{1,5},{2,6},{3,7},{4,0},{5,1},{6,2},{7,3},{8,12},{9,13},{10,... | collective-permute-start | bytes 921608 | tf_op jit(solution)/shard_map/ppermute | solution.py:522
  75.0 5.8 %collective-permute-done.23.b4 = bf16[48,3200]{1,0:T(8,128)(2,1)S(1)} collective-permute-done((bf16[48,3200]{1,0:T(8,128)(2,1)S(1)}, bf16[48,3200]{1,0:T(8,128)(2,1)S(1)}, u32[]{:S(2)}, u32[]{:S(2)}) %collective-permute-start.23) | collective-permute-done | bytes 307232 | tf_op jit(solution)/shard_map/ppermute | solution.py:522
  82.9 1.9 %collective-permute-start.27 = (bf16[48,3200]{1,0:T(8,128)(2,1)S(1)}, bf16[48,3200]{1,0:T(8,128)(2,1)S(1)}, u32[]{:S(2)}, u32[]{:S(2)}) collective-permute-start(bf16[48,3200]{1,0:T(8,128)(2,1)S(1)} %collective-permute-done.25.b2), channel_id=1, source_target_pairs={{0,4},{1,5},{2,6},{3,7},{4,0},{5,1},{6,2},{7,3},{8,12},{9,13},{10,... | collective-permute-start | bytes 921608 | tf_op jit(solution)/shard_map/ppermute | solution.py:526
  84.8 6.5 %collective-permute-done.27.b6 = bf16[48,3200]{1,0:T(8,128)(2,1)S(1)} collective-permute-done((bf16[48,3200]{1,0:T(8,128)(2,1)S(1)}, bf16[48,3200]{1,0:T(8,128)(2,1)S(1)}, u32[]{:S(2)}, u32[]{:S(2)}) %collective-permute-start.27) | collective-permute-done | bytes 307232 | tf_op jit(solution)/shard_map/ppermute | solution.py:526
  91.3 2.8 %collective-permute-done.26.below = bf16[96,3200]{1,0:T(8,128)(2,1)S(1)} collective-permute-done((bf16[96,3200]{1,0:T(8,128)(2,1)S(1)}, bf16[96,3200]{1,0:T(8,128)(2,1)S(1)}, u32[]{:S(2)}, u32[]{:S(2)}) %collective-permute-start.26) | collective-permute-done | bytes 614432 | tf_op jit(solution)/shard_map/ppermute | solution.py:524
  94.1 2.4 %collective-permute-done.24.above = bf16[96,3200]{1,0:T(8,128)(2,1)S(1)} collective-permute-done((bf16[96,3200]{1,0:T(8,128)(2,1)S(1)}, bf16[96,3200]{1,0:T(8,128)(2,1)S(1)}, u32[]{:S(2)}, u32[]{:S(2)}) %collective-permute-start.24) | collective-permute-done | bytes 614432 | tf_op jit(solution)/shard_map/ppermute | solution.py:525
  96.5 2.8 %normed.1 = (bf16[392,1024]{1,0:T(8,128)(2,1)S(1)}, bf16[384,1024]{1,0:T(8,128)(2,1)S(1)}, f32[8,1024]{1,0:T(8,128)S(1)}) custom-call(bf16[768,384]{1,0:T(8,128)(2,1)S(1)} %get-tuple-element.41.spread, bf16[48,3200]{1,0:T(8,128)(2,1)S(1)} %hidden.1.own, bf16[96,3200]{1,0:T(8,128)(2,1)S(1)} %collective-permute-done.24.above, ...), custom_call_target="tpu_custom_call" | custom-call | flops 2400000000 | bytes 9000000 | tf_op jit(solution)/shard_map/normed/pallas_call | solution.py:528
  101.9 3.3 %collective-permute-start.31 = (bf16[56,1024]{1,0:T(8,128)(2,1)S(1)}, bf16[56,1024]{1,0:T(8,128)(2,1)S(1)}, u32[]{:S(2)}, u32[]{:S(2)}) collective-permute-start(bf16[56,1024]{1,0:T(8,128)(2,1)S(1)} %get-tuple-element.62), channel_id=1, source_target_pairs={{0,32},{8,40},{16,48},{24,56},{32,64},{40,72},{48,80},{56,88},{64,... | collective-permute-start | bytes 344072 | tf_op jit(solution)/shard_map/ppermute | solution.py:42
  106.7 2.7 %convolution_convert_fusion.1 = bf16[1024,1024]{1,0:T(8,128)(2,1)} fusion(bf16[384,3200]{1,0:T(8,128)(2,1)S(1)} %slice_dynamic-update-slice_fusion, bf16[384,1024]{1,0:T(8,128)(2,1)S(1)} %get-tuple-element.55.sel, f32[1024]{0:T(1024)S(1)} %copy-done.10, f32[384]{0:T(512)S(1)} %get-tuple-element.75), kind=kOutput, calls=%fused_computation.1 | convolution fusion | flops 807927808 | bytes 3676160 | tf_op jit(solution)/shard_map/dot_general | solution.py:78
  109.9 2.8 %collective-permute-start.30 = (bf16[56,1024]{1,0:T(8,128)(2,1)S(1)}, bf16[56,1024]{1,0:T(8,128)(2,1)S(1)}, u32[]{:S(2)}, u32[]{:S(2)}) collective-permute-start(bf16[56,1024]{1,0:T(8,128)(2,1)S(1)} %get-tuple-element.61), channel_id=1, source_target_pairs={{0,224},{8,232},{16,240},{24,248},{32,0},{40,8},{48,16},{56,24},{6... | collective-permute-start | bytes 344072 | tf_op jit(solution)/shard_map/ppermute | solution.py:42
  114.4 4.1 %collective-permute-start.35 = (bf16[56,1024]{1,0:T(8,128)(2,1)S(1)}, bf16[56,1024]{1,0:T(8,128)(2,1)S(1)}, u32[]{:S(2)}, u32[]{:S(2)}) collective-permute-start(bf16[56,1024]{1,0:T(8,128)(2,1)S(1)} %get-tuple-element.66), channel_id=1, source_target_pairs={{0,192},{8,200},{16,208},{24,216},{32,224},{40,232},{48,240},{56,2... | collective-permute-start | bytes 344072 | tf_op jit(solution)/shard_map/ppermute | solution.py:42
  118.5 2.7 %convolution_convert_fusion.2 = bf16[1024,1024]{1,0:T(8,128)(2,1)} fusion(bf16[384,3200]{1,0:T(8,128)(2,1)S(1)} %slice_dynamic-update-slice_fusion, bf16[384,1024]{1,0:T(8,128)(2,1)S(1)} %get-tuple-element.55.sel, f32[1024]{0:T(1024)S(1)} %copy-done.10, f32[384]{0:T(512)S(1)} %get-tuple-element.75), kind=kOutput, calls=%fused_computation.2 | convolution fusion | flops 807927808 | bytes 3676160 | tf_op jit(solution)/shard_map/dot_general | solution.py:78
  122.8 2.7 %convolution_convert_fusion = bf16[1024,1024]{1,0:T(8,128)(2,1)} fusion(bf16[384,1024]{1,0:T(8,128)(2,1)S(1)} %get-tuple-element.71, bf16[384,3200]{1,0:T(8,128)(2,1)S(1)} %slice_dynamic-update-slice_fusion, f32[384]{0:T(512)S(1)} %get-tuple-element.74), kind=kOutput, calls=%fused_computation | convolution fusion | flops 807534592 | bytes 3672064 | tf_op jit(solution)/shard_map/dot_general | solution.py:78
  (102 shorter events, 42.2 us)
Async XLA Ops:
  7.6 18.8 %collective-permute-start.5 = (bf16[48,2048]{1,0:T(8,128)(2,1)S(1)}, bf16[48,2048]{1,0:T(8,128)(2,1)S(1)}, u32[]{:S(2)}, u32[]{:S(2)}) collective-permute-start(bf16[48,2048]{1,0:T(8,128)(2,1)S(1)} %constant_dynamic-update-slice_fusion.refs_3_), channel_id=1, source_target_pairs={{0,192},{8,200},{16,208},{24,216},{32,224},{40,232},{48,240},{56,2... | collective-permute-start | bytes 589832 | tf_op jit(solution)/shard_map/ppermute | solution.py:42
  14.0 13.0 %collective-permute-start.4 = (bf16[48,2048]{1,0:T(8,128)(2,1)S(1)}, bf16[48,2048]{1,0:T(8,128)(2,1)S(1)}, u32[]{:S(2)}, u32[]{:S(2)}) collective-permute-start(bf16[48,2048]{1,0:T(8,128)(2,1)S(1)} %constant_dynamic-update-slice_fusion.refs_3_), channel_id=1, source_target_pairs={{0,224},{8,232},{16,240},{24,248},{32,0},{40,8},{48,16},{56,24},{6... | collective-permute-start | bytes 589832 | tf_op jit(solution)/shard_map/ppermute | solution.py:42
  15.0 15.0 %collective-permute-start.1 = (bf16[48,2048]{1,0:T(8,128)(2,1)S(1)}, bf16[48,2048]{1,0:T(8,128)(2,1)S(1)}, u32[]{:S(2)}, u32[]{:S(2)}) collective-permute-start(bf16[48,2048]{1,0:T(8,128)(2,1)S(1)} %constant_dynamic-update-slice_fusion.refs_3_), channel_id=1, source_target_pairs={{0,64},{8,72},{16,80},{24,88},{32,96},{40,104},{48,112},{56,120},{... | collective-permute-start | bytes 589832 | tf_op jit(solution)/shard_map/ppermute | solution.py:42
  16.5 13.5 %collective-permute-start.11 = (bf16[48,2048]{1,0:T(8,128)(2,1)S(1)}, bf16[48,2048]{1,0:T(8,128)(2,1)S(1)}, u32[]{:S(2)}, u32[]{:S(2)}) collective-permute-start(bf16[48,2048]{1,0:T(8,128)(2,1)S(1)} %constant_dynamic-update-slice_fusion.refs_3_), channel_id=1, source_target_pairs={{0,8},{8,0},{16,24},{24,16},{32,40},{40,32},{48,56},{56,48},{64,72... | collective-permute-start | bytes 589832 | tf_op jit(solution)/shard_map/ppermute | solution.py:441
  16.5 13.6 %collective-permute-start.3 = (bf16[48,2048]{1,0:T(8,128)(2,1)S(1)}, bf16[48,2048]{1,0:T(8,128)(2,1)S(1)}, u32[]{:S(2)}, u32[]{:S(2)}) collective-permute-start(bf16[48,2048]{1,0:T(8,128)(2,1)S(1)} %constant_dynamic-update-slice_fusion.refs_3_), channel_id=1, source_target_pairs={{0,32},{8,40},{16,48},{24,56},{32,64},{40,72},{48,80},{56,88},{64,... | collective-permute-start | bytes 589832 | tf_op jit(solution)/shard_map/ppermute | solution.py:42
  27.0 8.8 %collective-permute-start.6 = (bf16[48,2048]{1,0:T(8,128)(2,1)S(1)}, bf16[48,2048]{1,0:T(8,128)(2,1)S(1)}, u32[]{:S(2)}, u32[]{:S(2)}) collective-permute-start(bf16[48,2048]{1,0:T(8,128)(2,1)S(1)} %collective-permute-done.5.above.refs_5_), channel_id=1, source_target_pairs={{0,224},{8,232},{16,240},{24,248},{32,0},{40,8},{48,16},{56,24},{6... | collective-permute-start | bytes 589832 | tf_op jit(solution)/shard_map/ppermute | solution.py:42
  30.0 10.7 %collective-permute-start.2 = (bf16[48,2048]{1,0:T(8,128)(2,1)S(1)}, bf16[48,2048]{1,0:T(8,128)(2,1)S(1)}, u32[]{:S(2)}, u32[]{:S(2)}) collective-permute-start(bf16[48,2048]{1,0:T(8,128)(2,1)S(1)} %collective-permute-done.1.below.refs_1_), channel_id=1, source_target_pairs={{0,32},{8,40},{16,48},{24,56},{32,64},{40,72},{48,80},{56,88},{64,... | collective-permute-start | bytes 589832 | tf_op jit(solution)/shard_map/ppermute | solution.py:42
  30.1 10.6 %collective-permute-start.7 = (bf16[48,2048]{1,0:T(8,128)(2,1)S(1)}, bf16[48,2048]{1,0:T(8,128)(2,1)S(1)}, u32[]{:S(2)}, u32[]{:S(2)}) collective-permute-start(bf16[48,2048]{1,0:T(8,128)(2,1)S(1)} %far.1), channel_id=1, source_target_pairs={{0,64},{8,200},{16,80},{24,216},{32,96},{40,232},{48,112},{56,248}... | collective-permute-start | bytes 589832 | tf_op jit(solution)/shard_map/ppermute | solution.py:439
  30.2 11.0 %collective-permute-start.9 = (bf16[48,2048]{1,0:T(8,128)(2,1)S(1)}, bf16[48,2048]{1,0:T(8,128)(2,1)S(1)}, u32[]{:S(2)}, u32[]{:S(2)}) collective-permute-start(bf16[48,2048]{1,0:T(8,128)(2,1)S(1)} %collective-permute-done.1.below.refs_1_), channel_id=1, source_target_pairs={{0,8},{8,0},{16,24},{24,16},{32,40},{40,32},{48,56},{56,48},{64,72... | collective-permute-start | bytes 589832 | tf_op jit(solution)/shard_map/ppermute | solution.py:441
  46.6 10.2 %collective-permute-start.18 = (bf16[48,3200]{1,0:T(8,128)(2,1)S(1)}, bf16[48,3200]{1,0:T(8,128)(2,1)S(1)}, u32[]{:S(2)}, u32[]{:S(2)}) collective-permute-start(bf16[48,3200]{1,0:T(8,128)(2,1)S(1)} %get-tuple-element.50), channel_id=1, source_target_pairs={{0,1},{1,2},{2,3},{3,0},{4,5},{5,6},{6,7},{7,4},{8,9},{9,10},{10,1... | collective-permute-start | bytes 921608 | tf_op jit(solution)/shard_map/ppermute | solution.py:498
  47.1 11.4 %collective-permute-start.19 = (bf16[48,3200]{1,0:T(8,128)(2,1)S(1)}, bf16[48,3200]{1,0:T(8,128)(2,1)S(1)}, u32[]{:S(2)}, u32[]{:S(2)}) collective-permute-start(bf16[48,3200]{1,0:T(8,128)(2,1)S(1)} %get-tuple-element.51), channel_id=1, source_target_pairs={{0,3},{1,0},{2,1},{3,2},{4,7},{5,4},{6,5},{7,6},{8,11},{9,8},{10,9... | collective-permute-start | bytes 921608 | tf_op jit(solution)/shard_map/ppermute | solution.py:499
  48.7 10.4 %collective-permute-start.20 = (bf16[48,3200]{1,0:T(8,128)(2,1)S(1)}, bf16[48,3200]{1,0:T(8,128)(2,1)S(1)}, u32[]{:S(2)}, u32[]{:S(2)}) collective-permute-start(bf16[48,3200]{1,0:T(8,128)(2,1)S(1)} %get-tuple-element.52), channel_id=1, source_target_pairs={{0,4},{1,5},{2,6},{3,7},{4,0},{5,1},{6,2},{7,3},{8,12},{9,13},{10,... | collective-permute-start | bytes 921608 | tf_op jit(solution)/shard_map/ppermute | solution.py:500
  49.0 14.3 %collective-permute-start.16 = (bf16[48,3200]{1,0:T(8,128)(2,1)S(1)}, bf16[48,3200]{1,0:T(8,128)(2,1)S(1)}, u32[]{:S(2)}, u32[]{:S(2)}) collective-permute-start(bf16[48,3200]{1,0:T(8,128)(2,1)S(1)} %get-tuple-element.48), channel_id=1, source_target_pairs={{0,1},{1,2},{2,3},{3,0},{4,5},{5,6},{6,7},{7,4},{8,9},{9,10},{10,1... | collective-permute-start | bytes 921608 | tf_op jit(solution)/shard_map/ppermute | solution.py:501
  50.7 19.9 %collective-permute-start.17 = (bf16[48,3200]{1,0:T(8,128)(2,1)S(1)}, bf16[48,3200]{1,0:T(8,128)(2,1)S(1)}, u32[]{:S(2)}, u32[]{:S(2)}) collective-permute-start(bf16[48,3200]{1,0:T(8,128)(2,1)S(1)} %get-tuple-element.49), channel_id=1, source_target_pairs={{0,3},{1,0},{2,1},{3,2},{4,7},{5,4},{6,5},{7,6},{8,11},{9,8},{10,9... | collective-permute-start | bytes 921608 | tf_op jit(solution)/shard_map/ppermute | solution.py:501
  59.7 10.9 %collective-permute-start.21 = (bf16[48,3200]{1,0:T(8,128)(2,1)S(1)}, bf16[48,3200]{1,0:T(8,128)(2,1)S(1)}, u32[]{:S(2)}, u32[]{:S(2)}) collective-permute-start(bf16[48,3200]{1,0:T(8,128)(2,1)S(1)} %get-tuple-element.53), channel_id=1, source_target_pairs={{0,4},{1,5},{2,6},{3,7},{4,0},{5,1},{6,2},{7,3},{8,12},{9,13},{10,... | collective-permute-start | bytes 921608 | tf_op jit(solution)/shard_map/ppermute | solution.py:511
  60.1 10.5 %collective-permute-start.22 = (bf16[48,3200]{1,0:T(8,128)(2,1)S(1)}, bf16[48,3200]{1,0:T(8,128)(2,1)S(1)}, u32[]{:S(2)}, u32[]{:S(2)}) collective-permute-start(bf16[48,3200]{1,0:T(8,128)(2,1)S(1)} %get-tuple-element.54), channel_id=1, source_target_pairs={{0,2},{1,3},{2,0},{3,1},{4,6},{5,7},{6,4},{7,5},{8,10},{9,11},{10,... | collective-permute-start | bytes 921608 | tf_op jit(solution)/shard_map/ppermute | solution.py:510
  71.6 9.1 %collective-permute-start.23 = (bf16[48,3200]{1,0:T(8,128)(2,1)S(1)}, bf16[48,3200]{1,0:T(8,128)(2,1)S(1)}, u32[]{:S(2)}, u32[]{:S(2)}) collective-permute-start(bf16[48,3200]{1,0:T(8,128)(2,1)S(1)} %hidden.1.own), channel_id=1, source_target_pairs={{0,4},{1,5},{2,6},{3,7},{4,0},{5,1},{6,2},{7,3},{8,12},{9,13},{10,... | collective-permute-start | bytes 921608 | tf_op jit(solution)/shard_map/ppermute | solution.py:522
  73.6 9.3 %collective-permute-start.25 = (bf16[48,3200]{1,0:T(8,128)(2,1)S(1)}, bf16[48,3200]{1,0:T(8,128)(2,1)S(1)}, u32[]{:S(2)}, u32[]{:S(2)}) collective-permute-start(bf16[48,3200]{1,0:T(8,128)(2,1)S(1)} %hidden.1.own), channel_id=1, source_target_pairs={{0,2},{1,3},{2,0},{3,1},{4,6},{5,7},{6,4},{7,5},{8,10},{9,11},{10,... | collective-permute-start | bytes 921608 | tf_op jit(solution)/shard_map/ppermute | solution.py:521
  80.8 13.3 %collective-permute-start.26 = (bf16[96,3200]{1,0:T(8,128)(2,1)S(1)}, bf16[96,3200]{1,0:T(8,128)(2,1)S(1)}, u32[]{:S(2)}, u32[]{:S(2)}) collective-permute-start(bf16[96,3200]{1,0:T(8,128)(2,1)S(1)} %pad_maximum_fusion), channel_id=1, source_target_pairs={{0,1},{1,2},{2,3},{3,0},{4,5},{5,6},{6,7},{7,4},{8,9},{9,10},{10,1... | collective-permute-start | bytes 1843208 | tf_op jit(solution)/shard_map/ppermute | solution.py:524
  82.3 14.2 %collective-permute-start.24 = (bf16[96,3200]{1,0:T(8,128)(2,1)S(1)}, bf16[96,3200]{1,0:T(8,128)(2,1)S(1)}, u32[]{:S(2)}, u32[]{:S(2)}) collective-permute-start(bf16[96,3200]{1,0:T(8,128)(2,1)S(1)} %pad_maximum_fusion), channel_id=1, source_target_pairs={{0,3},{1,0},{2,1},{3,2},{4,7},{5,4},{6,5},{7,6},{8,11},{9,8},{10,9... | collective-permute-start | bytes 1843208 | tf_op jit(solution)/shard_map/ppermute | solution.py:525
  101.9 10.8 %collective-permute-start.31 = (bf16[56,1024]{1,0:T(8,128)(2,1)S(1)}, bf16[56,1024]{1,0:T(8,128)(2,1)S(1)}, u32[]{:S(2)}, u32[]{:S(2)}) collective-permute-start(bf16[56,1024]{1,0:T(8,128)(2,1)S(1)} %get-tuple-element.62), channel_id=1, source_target_pairs={{0,32},{8,40},{16,48},{24,56},{32,64},{40,72},{48,80},{56,88},{64,... | collective-permute-start | bytes 344072 | tf_op jit(solution)/shard_map/ppermute | solution.py:42
  105.2 8.9 %collective-permute-start.33 = (bf16[56,1024]{1,0:T(8,128)(2,1)S(1)}, bf16[56,1024]{1,0:T(8,128)(2,1)S(1)}, u32[]{:S(2)}, u32[]{:S(2)}) collective-permute-start(bf16[56,1024]{1,0:T(8,128)(2,1)S(1)} %get-tuple-element.64), channel_id=1, source_target_pairs={{0,64},{8,200},{16,80},{24,216},{32,96},{40,232},{48,112},{56,248}... | collective-permute-start | bytes 344072 | tf_op jit(solution)/shard_map/ppermute | solution.py:561
  109.4 11.8 %collective-permute-start.29 = (bf16[56,1024]{1,0:T(8,128)(2,1)S(1)}, bf16[56,1024]{1,0:T(8,128)(2,1)S(1)}, u32[]{:S(2)}, u32[]{:S(2)}) collective-permute-start(bf16[56,1024]{1,0:T(8,128)(2,1)S(1)} %get-tuple-element.60), channel_id=1, source_target_pairs={{0,32},{8,40},{16,48},{24,56},{32,64},{40,72},{48,80},{56,88},{64,... | collective-permute-start | bytes 344072 | tf_op jit(solution)/shard_map/ppermute | solution.py:42
  109.9 11.3 %collective-permute-start.30 = (bf16[56,1024]{1,0:T(8,128)(2,1)S(1)}, bf16[56,1024]{1,0:T(8,128)(2,1)S(1)}, u32[]{:S(2)}, u32[]{:S(2)}) collective-permute-start(bf16[56,1024]{1,0:T(8,128)(2,1)S(1)} %get-tuple-element.61), channel_id=1, source_target_pairs={{0,224},{8,232},{16,240},{24,248},{32,0},{40,8},{48,16},{56,24},{6... | collective-permute-start | bytes 344072 | tf_op jit(solution)/shard_map/ppermute | solution.py:42
  (25 other events, 168.6 us)
where the time goes:
time: 130 us; the launch traced here: 129 us
  waiting for transfers between devices  52.1 us (40%)
  starting transfers between devices  43.3 us (33%)
  Pallas kernels  14.8 us (11%)
  local copies, waits for them, and re-layouts  9.03 us (7%)
  matrix products  8.09 us (6%)
    ppermute x12, starting transfers between devices, along(): lax.ppermute(value, 'wide', wide_pairs(lambda z, y, c: (z + 8 + step, y,...  22.7 us
    ppermute x12, waiting for transfers between devices, along(): lax.ppermute(value, 'wide', wide_pairs(lambda z, y, c: (z + 8 + step, y,...  9 us
    unnamed x32, local copies, waits for them, and re-layouts  8.2 us
    dot_general x3, matrix products, mm(): lax.dot_general(a, b, (((ca,), (cb,)), ((), ())), preferred_element_type=...  8.09 us
    ppermute x1, waiting for transfers between devices, local(): lax.ppermute(near[1], 'narrow', XDOWN)  7.3 us
    ppermute x1, waiting for transfers between devices, local(): b6 = lax.ppermute(b2, 'narrow', YHI)  6.45 us
    ppermute x1, waiting for transfers between devices, local(): b4 = lax.ppermute(own, 'narrow', YHI)  5.79 us
    ppermute x1, waiting for transfers between devices, local(): from_below = lax.ppermute(to_up, 'narrow', XUP)  5.71 us
  transfers between devices with their start and end apart: 37, of which 18 were waited for; matrix products, arithmetic and copies ran while one was open for 8% of the time, Pallas kernels for 2%

commit v1 on v0

--- a/solution.py
+++ b/solution.py
@@ -139,19 +139,32 @@
         out[:, n * W : n * W + W] = mm(pick, held[...], 0, 0).astype(bf16)
 
 
-def onehot_kernel(sel_col, gain, rw, _, *refs):
-    weights, (put, spread, vectors), held, sems = refs[:3], refs[3:6], refs[6:9], refs[9]
-    loads = [pltpu.make_async_copy(weights[n], held[n], sems.at[n]) for n in range(3)]
+def onehot_kernel(sel_row, *refs):
+    sources, (put, spread, vectors), held, sems = refs[:2], refs[2:5], refs[5:7], refs[7]
+    loads = [pltpu.make_async_copy(sources[n], held[n], sems.at[n]) for n in range(2)]
     for load in loads:
         load.start()
-    vectors[0:1, :] = gain[...]
-    vectors[1:2, :] = rw[...]
+    eye = lax.broadcasted_iota(i32, (SEL, SEL), 0) == lax.broadcasted_iota(i32, (SEL, SEL), 1)
+    sel_col = jnp.sum(jnp.where(eye, sel_row[...], 0), axis=1, keepdims=True)
+
     @pl.loop(0, 2 * SEL // 128)
     def _(i):
-        hot = placement(sel_col[...], i * 128, 128)
+        hot = placement(sel_col, i * 128, 128)
         put[:, span(i, 128)] = hot.astype(bf16)
         spread[span(i, 128), :] = hot.T.astype(bf16)
 
+    for load in loads:
+        load.wait()
+    vectors[0:1, :] = held[0][...]
+    vectors[1:2, :] = held[1][...]
+
+
+def stage_kernel(*refs):
+    sources, piece, held, out, sems = refs[:3], refs[3], refs[5:8], refs[8], refs[9]
+    loads = [pltpu.make_async_copy(sources[n], held[n], sems.at[n]) for n in range(3)]
+    for load in loads:
+        load.start()
+    out[...] = piece[...]
     for load in loads:
         load.wait()
 
@@ -220,9 +233,9 @@
         (to_far, (keep.at[96:144], from_y)),
     ):
 
-        @pl.loop(0, 3 * W // TILE)
+        @pl.loop(0, 3 * W // WIDER)
         def _(k, out=out, refs=refs):
-            cols = span(k, TILE)
+            cols = span(k, WIDER)
             total = refs[0][:, cols].astype(f32)
             for ref in refs[1:]:
                 total = total + ref[:, cols].astype(f32)
@@ -243,7 +256,7 @@
         router_grad, inner = carry
 
         def total(start):
-            cols = span(i, TILE, start)
+            cols = span(i, WIDER, start)
             value = refs[0][:, cols].astype(f32)
             for ref in refs[1:]:
                 value = value + ref[:, cols].astype(f32)
@@ -261,13 +274,13 @@
         inner += jnp.sum(
             d_gate.astype(f32) * gate + d_up.astype(f32) * upv, axis=1, keepdims=True
         )
-        out[:, span(i, TILE)] = d_gate
-        out[:, span(i, TILE, W)] = d_up
-        out[:, span(i, TILE, 2 * W)] = hidden
+        out[:, span(i, WIDER)] = d_gate
+        out[:, span(i, WIDER, W)] = d_up
+        out[:, span(i, WIDER, 2 * W)] = hidden
         return router_grad, inner
 
     zero = jnp.zeros((rows, 1), f32)
-    router_grad, inner = lax.fori_loop(0, W // TILE, tile, (zero, zero))
+    router_grad, inner = lax.fori_loop(0, W // WIDER, tile, (zero, zero))
     out[:, 3 * W :] = lanes_of(
         heads(scale, 3) + heads(logit, 3) + heads(router_grad, 3) + heads(inner, 3), rows
     )
@@ -421,13 +434,11 @@
         grad_x[:, cols] = (go[:, cols].astype(f32) + spread).astype(bf16)
 
 
-def gather(pair, after):
+def gather(pair, after, *weights):
     held = {0: pair}
-    for k in (2, 1):
-        held[-k] = along(pair, k)
-        held[k] = along(pair, -k)
-    held[-3] = along(held[-2], 1)
-    held[3] = along(held[2], -1)
+    for k in (1, 2, 3):
+        held[-k] = along(held[1 - k], 1)
+        held[k] = along(held[k - 1], -1)
     far = pl.pallas_call(
         far_kernel,
         out_shape=jax.ShapeDtypeStruct(pair.shape, bf16),
@@ -437,12 +448,23 @@
         name="far",
     )(held[-2], held[2], after)
     held[4] = lax.ppermute(far, "wide", ZFAR)
+    anywhere = pl.BlockSpec(memory_space=pl.ANY)
+    *weights, above = pl.pallas_call(
+        stage_kernel,
+        out_shape=(jax.ShapeDtypeStruct((W, W), bf16),) * 3
+        + (jax.ShapeDtypeStruct(pair.shape, bf16),),
+        in_specs=[anywhere] * 3 + [VMEM, anywhere],
+        out_specs=(VMEM,) * 4,
+        scratch_shapes=[pltpu.SemaphoreType.DMA((3,))],
+        compiler_params=params(16),
+        name="stage",
+    )(*weights, held[2], far)
     ours = [held[k] for k in range(-3, 5)]
-    return ours + [lax.ppermute(piece, "wide", CORE) for piece in ours]
+    sent = ours[:5] + [above] + ours[6:]
+    return ours + [lax.ppermute(piece, "wide", CORE) for piece in sent], weights
 
 
 def local(tokens, grad_out, selected, gain, router_weight, w_gate, w_up, w_down):
-    sel_col = selected.reshape(SEL, 1)
     gain = gain.reshape(1, W)
     router_weight = router_weight.reshape(1, W)
     anywhere = pl.BlockSpec(memory_space=pl.ANY)
@@ -460,22 +482,21 @@
         compiler_params=params(60),
         name="own",
     )(selected, tokens, grad_out)
-    put, spread, vectors, *weights = pl.pallas_call(
+    put, spread, vectors = pl.pallas_call(
         onehot_kernel,
         out_shape=(
             jax.ShapeDtypeStruct((SEL, 2 * SEL), bf16),
             jax.ShapeDtypeStruct((2 * SEL, SEL), bf16),
             jax.ShapeDtypeStruct((2, W), f32),
-        )
-        + (jax.ShapeDtypeStruct((W, W), bf16),) * 3,
-        in_specs=[VMEM] * 3 + [anywhere] * 4,
-        out_specs=(VMEM,) * 6,
-        scratch_shapes=[pltpu.SemaphoreType.DMA((3,))],
+        ),
+        in_specs=[VMEM] + [anywhere] * 2,
+        out_specs=(VMEM,) * 3,
+        scratch_shapes=[pltpu.VMEM((1, W), f32)] * 2 + [pltpu.SemaphoreType.DMA((2,))],
         compiler_params=params(16),
         name="onehot",
-    )(sel_col, gain, router_weight, mine, w_gate, w_up, w_down)
+    )(sel_row, gain, router_weight)
     pair = jnp.concatenate([mine, lax.ppermute(mine, "wide", YLO)], axis=0)
-    parts = gather(pair, put)
+    parts, weights = gather(pair, put, w_gate, w_up, w_down)
 
     full = lambda *shape: pl.BlockSpec(shape, lambda j: (0,) * len(shape))
     block = jax.ShapeDtypeStruct((48, ROW), bf16)

time: 130 us -> 127 us (0.977)
  waiting for transfers between devices: 52.1 us -> 49.6 us
    ppermute x1, waiting for transfers between devices: 1.44 us -> 0.01 us  [local(): far = lax.ppermute(far, 'wide', ZFAR)]
    ppermute x12, waiting for transfers between devices: 9 us -> 7.59 us  [along(): lax.ppermute(value, 'wide', wide_pairs(lambda z, y, c: (z + 8 + step, y,...]
  transfers between devices with their start and end apart: 37 -> 37, of which waited for: 18 -> 17; matrix products, arithmetic and copies ran while one was open for 8% -> 8% of each run, Pallas kernels for 2% -> 2%
where the time goes in v1:
time: 127 us; the launch traced here: 125 us
  waiting for transfers between devices  49.6 us (39%)
  starting transfers between devices  43.5 us (34%)
  Pallas kernels  14.6 us (11%)
  matrix products  8.06 us (6%)
  local copies, waits for them, and re-layouts  8.02 us (6%)
    ppermute x12, starting transfers between devices, along(): lax.ppermute(value, 'wide', wide_pairs(lambda z, y, c: (z + 8 + step, y,...  23.6 us
    dot_general x3, matrix products, mm(): lax.dot_general(a, b, (((ca,), (cb,)), ((), ())), preferred_element_type=...  8.06 us
    unnamed x32, local copies, waits for them, and re-layouts  7.99 us
    ppermute x12, waiting for transfers between devices, along(): lax.ppermute(value, 'wide', wide_pairs(lambda z, y, c: (z + 8 + step, y,...  7.59 us
    ppermute x1, waiting for transfers between devices, local(): lax.ppermute(near[1], 'narrow', XDOWN)  7.3 us
    ppermute x1, waiting for transfers between devices, local(): b6 = lax.ppermute(b2, 'narrow', YHI)  6.52 us
    ppermute x1, waiting for transfers between devices, local(): b4 = lax.ppermute(own, 'narrow', YHI)  5.92 us
    ppermute x1, waiting for transfers between devices, local(): from_below = lax.ppermute(to_up, 'narrow', XUP)  5.71 us
  transfers between devices with their start and end apart: 37, of which 17 were waited for; matrix products, arithmetic and copies ran while one was open for 8% of the time, Pallas kernels for 2%

profile of v1, /device:TPU:22, one launch (start us, length us, event | category | flops | bytes accessed | tf_op | source)
XLA Modules:
  0.0 125.0 jit_solution(17678154082619442680)
XLA Ops:
  0.6 2.0 %own.1 = (bf16[24,2048]{1,0:T(8,128)(2,1)}, s32[1,384]{1,0:T(1,128)}) custom-call(s32[384]{0:T(512)} %sel_hbm.1, bf16[96,1024]{1,0:T(8,128)(2,1)} %tok_hbm.1, bf16[96,1024]{1,0:T(8,128)(2,1)} %go.1), custom_call_target="tpu_custom_call" | custom-call | tf_op jit(solution)/shard_map/own/pallas_call | solution.py:471
  5.0 2.6 %collective-permute-done = bf16[24,2048]{1,0:T(8,128)(2,1)S(1)} collective-permute-done((bf16[24,2048]{1,0:T(8,128)(2,1)}, bf16[24,2048]{1,0:T(8,128)(2,1)S(1)}, u32[]{:S(2)}, u32[]{:S(2)}) %collective-permute-start) | collective-permute-done | bytes 98336 | tf_op jit(solution)/shard_map/ppermute | solution.py:498
  7.6 5.9 %collective-permute-start.4 = (bf16[48,2048]{1,0:T(8,128)(2,1)S(1)}, bf16[48,2048]{1,0:T(8,128)(2,1)S(1)}, u32[]{:S(2)}, u32[]{:S(2)}) collective-permute-start(bf16[48,2048]{1,0:T(8,128)(2,1)S(1)} %constant_dynamic-update-slice_fusion.refs_3_), channel_id=1, source_target_pairs={{0,224},{8,232},{16,240},{24,248},{32,0},{40,8},{48,16},{56,24},{6... | collective-permute-start | bytes 589832 | tf_op jit(solution)/shard_map/ppermute | solution.py:42
  13.5 3.2 %collective-permute-done.4.refs_4_ = bf16[48,2048]{1,0:T(8,128)(2,1)S(1)} collective-permute-done((bf16[48,2048]{1,0:T(8,128)(2,1)S(1)}, bf16[48,2048]{1,0:T(8,128)(2,1)S(1)}, u32[]{:S(2)}, u32[]{:S(2)}) %collective-permute-start.4) | collective-permute-done | bytes 196640 | tf_op jit(solution)/shard_map/ppermute | solution.py:42
  16.7 3.7 %collective-permute-start.5 = (bf16[48,2048]{1,0:T(8,128)(2,1)S(1)}, bf16[48,2048]{1,0:T(8,128)(2,1)S(1)}, u32[]{:S(2)}, u32[]{:S(2)}) collective-permute-start(bf16[48,2048]{1,0:T(8,128)(2,1)S(1)} %collective-permute-done.4.refs_4_), channel_id=1, source_target_pairs={{0,224},{8,232},{16,240},{24,248},{32,0},{40,8},{48,16},{56,24},{6... | collective-permute-start | bytes 589832 | tf_op jit(solution)/shard_map/ppermute | solution.py:42
  24.8 3.2 %collective-permute-start.6 = (bf16[48,2048]{1,0:T(8,128)(2,1)S(1)}, bf16[48,2048]{1,0:T(8,128)(2,1)S(1)}, u32[]{:S(2)}, u32[]{:S(2)}) collective-permute-start(bf16[48,2048]{1,0:T(8,128)(2,1)S(1)} %collective-permute-done.5.above.refs_3_.refs_5_), channel_id=1, source_target_pairs={{0,224},{8,232},{16,240},{24,248},{32,0},{40,8},{48,16},{56,24},{6... | collective-permute-start | bytes 589832 | tf_op jit(solution)/shard_map/ppermute | solution.py:42
  35.5 2.9 %collective-permute-done.3.refs_0_ = bf16[48,2048]{1,0:T(8,128)(2,1)S(1)} collective-permute-done((bf16[48,2048]{1,0:T(8,128)(2,1)S(1)}, bf16[48,2048]{1,0:T(8,128)(2,1)S(1)}, u32[]{:S(2)}, u32[]{:S(2)}) %collective-permute-start.3) | collective-permute-done | bytes 196640 | tf_op jit(solution)/shard_map/ppermute | solution.py:42
  40.1 4.1 %forward.1 = (bf16[384,1024]{1,0:T(8,128)(2,1)S(1)}, bf16[384,1024]{1,0:T(8,128)(2,1)S(1)}, bf16[144,3200]{1,0:T(8,128)(2,1)S(1)}, bf16[48,3200]{1,0:T(8,128)(2,...) custom-call(bf16[48,2048]{1,0:T(8,128)(2,1)S(1)} %collective-permute, ...), custom_call_target="tpu_custom_call" | custom-call | flops 3600000000 | bytes 16000000 | tf_op jit(solution)/shard_map/forward/pallas_call | solution.py:503
  48.7 5.7 %collective-permute-done.18.from_below = bf16[48,3200]{1,0:T(8,128)(2,1)S(1)} collective-permute-done((bf16[48,3200]{1,0:T(8,128)(2,1)S(1)}, bf16[48,3200]{1,0:T(8,128)(2,1)S(1)}, u32[]{:S(2)}, u32[]{:S(2)}) %collective-permute-start.18) | collective-permute-done | bytes 307232 | tf_op jit(solution)/shard_map/ppermute | solution.py:519
  59.1 1.9 %collective-permute-done.16.near_below = bf16[48,3200]{1,0:T(8,128)(2,1)S(1)} collective-permute-done((bf16[48,3200]{1,0:T(8,128)(2,1)S(1)}, bf16[48,3200]{1,0:T(8,128)(2,1)S(1)}, u32[]{:S(2)}, u32[]{:S(2)}) %collective-permute-start.16) | collective-permute-done | bytes 307232 | tf_op jit(solution)/shard_map/ppermute | solution.py:522
  61.0 7.3 %collective-permute-done.17.near_above = bf16[48,3200]{1,0:T(8,128)(2,1)S(1)} collective-permute-done((bf16[48,3200]{1,0:T(8,128)(2,1)S(1)}, bf16[48,3200]{1,0:T(8,128)(2,1)S(1)}, u32[]{:S(2)}, u32[]{:S(2)}) %collective-permute-start.17) | collective-permute-done | bytes 307232 | tf_op jit(solution)/shard_map/ppermute | solution.py:522
  69.0 1.9 %collective-permute-start.23 = (bf16[48,3200]{1,0:T(8,128)(2,1)S(1)}, bf16[48,3200]{1,0:T(8,128)(2,1)S(1)}, u32[]{:S(2)}, u32[]{:S(2)}) collective-permute-start(bf16[48,3200]{1,0:T(8,128)(2,1)S(1)} %hidden.1.own), channel_id=1, source_target_pairs={{0,4},{1,5},{2,6},{3,7},{4,0},{5,1},{6,2},{7,3},{8,12},{9,13},{10,... | collective-permute-start | bytes 921608 | tf_op jit(solution)/shard_map/ppermute | solution.py:543
  72.3 5.9 %collective-permute-done.23.b4 = bf16[48,3200]{1,0:T(8,128)(2,1)S(1)} collective-permute-done((bf16[48,3200]{1,0:T(8,128)(2,1)S(1)}, bf16[48,3200]{1,0:T(8,128)(2,1)S(1)}, u32[]{:S(2)}, u32[]{:S(2)}) %collective-permute-start.23) | collective-permute-done | bytes 307232 | tf_op jit(solution)/shard_map/ppermute | solution.py:543
  80.4 1.8 %collective-permute-start.27 = (bf16[48,3200]{1,0:T(8,128)(2,1)S(1)}, bf16[48,3200]{1,0:T(8,128)(2,1)S(1)}, u32[]{:S(2)}, u32[]{:S(2)}) collective-permute-start(bf16[48,3200]{1,0:T(8,128)(2,1)S(1)} %collective-permute-done.25.b2), channel_id=1, source_target_pairs={{0,4},{1,5},{2,6},{3,7},{4,0},{5,1},{6,2},{7,3},{8,12},{9,13},{10,... | collective-permute-start | bytes 921608 | tf_op jit(solution)/shard_map/ppermute | solution.py:547
  82.2 6.5 %collective-permute-done.27.b6 = bf16[48,3200]{1,0:T(8,128)(2,1)S(1)} collective-permute-done((bf16[48,3200]{1,0:T(8,128)(2,1)S(1)}, bf16[48,3200]{1,0:T(8,128)(2,1)S(1)}, u32[]{:S(2)}, u32[]{:S(2)}) %collective-permute-start.27) | collective-permute-done | bytes 307232 | tf_op jit(solution)/shard_map/ppermute | solution.py:547
  88.8 2.9 %collective-permute-done.26.below = bf16[96,3200]{1,0:T(8,128)(2,1)S(1)} collective-permute-done((bf16[96,3200]{1,0:T(8,128)(2,1)S(1)}, bf16[96,3200]{1,0:T(8,128)(2,1)S(1)}, u32[]{:S(2)}, u32[]{:S(2)}) %collective-permute-start.26) | collective-permute-done | bytes 614432 | tf_op jit(solution)/shard_map/ppermute | solution.py:545
  91.7 2.4 %collective-permute-done.24.above = bf16[96,3200]{1,0:T(8,128)(2,1)S(1)} collective-permute-done((bf16[96,3200]{1,0:T(8,128)(2,1)S(1)}, bf16[96,3200]{1,0:T(8,128)(2,1)S(1)}, u32[]{:S(2)}, u32[]{:S(2)}) %collective-permute-start.24) | collective-permute-done | bytes 614432 | tf_op jit(solution)/shard_map/ppermute | solution.py:546
  94.0 2.8 %normed.1 = (bf16[392,1024]{1,0:T(8,128)(2,1)S(1)}, bf16[384,1024]{1,0:T(8,128)(2,1)S(1)}, f32[8,1024]{1,0:T(8,128)S(1)}) custom-call(bf16[768,384]{1,0:T(8,128)(2,1)S(1)} %get-tuple-element.42.spread, bf16[48,3200]{1,0:T(8,128)(2,1)S(1)} %hidden.1.own, bf16[96,3200]{1,0:T(8,128)(2,1)S(1)} %collective-permute-done.24.above, ...), custom_call_target="tpu_custom_call" | custom-call | flops 2400000000 | bytes 9000000 | tf_op jit(solution)/shard_map/normed/pallas_call | solution.py:549
  99.4 3.3 %collective-permute-start.31 = (bf16[56,1024]{1,0:T(8,128)(2,1)S(1)}, bf16[56,1024]{1,0:T(8,128)(2,1)S(1)}, u32[]{:S(2)}, u32[]{:S(2)}) collective-permute-start(bf16[56,1024]{1,0:T(8,128)(2,1)S(1)} %get-tuple-element.65), channel_id=1, source_target_pairs={{0,32},{8,40},{16,48},{24,56},{32,64},{40,72},{48,80},{56,88},{64,... | collective-permute-start | bytes 344072 | tf_op jit(solution)/shard_map/ppermute | solution.py:42
  104.2 2.7 %convolution_convert_fusion.1 = bf16[1024,1024]{1,0:T(8,128)(2,1)} fusion(bf16[384,3200]{1,0:T(8,128)(2,1)S(1)} %slice_dynamic-update-slice_fusion, bf16[384,1024]{1,0:T(8,128)(2,1)S(1)} %get-tuple-element.58.sel, f32[1024]{0:T(1024)S(1)} %copy-done.11, f32[384]{0:T(512)S(1)} %get-tuple-element.77), kind=kOutput, calls=%fused_computation.1 | convolution fusion | flops 807927808 | bytes 3676160 | tf_op jit(solution)/shard_map/dot_general | solution.py:78
  107.4 2.8 %collective-permute-start.30 = (bf16[56,1024]{1,0:T(8,128)(2,1)S(1)}, bf16[56,1024]{1,0:T(8,128)(2,1)S(1)}, u32[]{:S(2)}, u32[]{:S(2)}) collective-permute-start(bf16[56,1024]{1,0:T(8,128)(2,1)S(1)} %get-tuple-element.64), channel_id=1, source_target_pairs={{0,224},{8,232},{16,240},{24,248},{32,0},{40,8},{48,16},{56,24},{6... | collective-permute-start | bytes 344072 | tf_op jit(solution)/shard_map/ppermute | solution.py:42
  110.5 4.1 %collective-permute-start.35 = (bf16[56,1024]{1,0:T(8,128)(2,1)S(1)}, bf16[56,1024]{1,0:T(8,128)(2,1)S(1)}, u32[]{:S(2)}, u32[]{:S(2)}) collective-permute-start(bf16[56,1024]{1,0:T(8,128)(2,1)S(1)} %get-tuple-element.69), channel_id=1, source_target_pairs={{0,192},{8,200},{16,208},{24,216},{32,224},{40,232},{48,240},{56,2... | collective-permute-start | bytes 344072 | tf_op jit(solution)/shard_map/ppermute | solution.py:42
  114.6 2.7 %convolution_convert_fusion.2 = bf16[1024,1024]{1,0:T(8,128)(2,1)} fusion(bf16[384,3200]{1,0:T(8,128)(2,1)S(1)} %slice_dynamic-update-slice_fusion, bf16[384,1024]{1,0:T(8,128)(2,1)S(1)} %get-tuple-element.58.sel, f32[1024]{0:T(1024)S(1)} %copy-done.11, f32[384]{0:T(512)S(1)} %get-tuple-element.77), kind=kOutput, calls=%fused_computation.2 | convolution fusion | flops 807927808 | bytes 3676160 | tf_op jit(solution)/shard_map/dot_general | solution.py:78
  119.1 2.7 %convolution_convert_fusion = bf16[1024,1024]{1,0:T(8,128)(2,1)} fusion(bf16[384,1024]{1,0:T(8,128)(2,1)S(1)} %get-tuple-element.73, bf16[384,3200]{1,0:T(8,128)(2,1)S(1)} %slice_dynamic-update-slice_fusion, f32[384]{0:T(512)S(1)} %get-tuple-element.76), kind=kOutput, calls=%fused_computation | convolution fusion | flops 807534592 | bytes 3672064 | tf_op jit(solution)/shard_map/dot_general | solution.py:78
  (102 shorter events, 39.1 us)
Async XLA Ops:
  7.6 9.1 %collective-permute-start.4 = (bf16[48,2048]{1,0:T(8,128)(2,1)S(1)}, bf16[48,2048]{1,0:T(8,128)(2,1)S(1)}, u32[]{:S(2)}, u32[]{:S(2)}) collective-permute-start(bf16[48,2048]{1,0:T(8,128)(2,1)S(1)} %constant_dynamic-update-slice_fusion.refs_3_), channel_id=1, source_target_pairs={{0,224},{8,232},{16,240},{24,248},{32,0},{40,8},{48,16},{56,24},{6... | collective-permute-start | bytes 589832 | tf_op jit(solution)/shard_map/ppermute | solution.py:42
  16.7 8.1 %collective-permute-start.5 = (bf16[48,2048]{1,0:T(8,128)(2,1)S(1)}, bf16[48,2048]{1,0:T(8,128)(2,1)S(1)}, u32[]{:S(2)}, u32[]{:S(2)}) collective-permute-start(bf16[48,2048]{1,0:T(8,128)(2,1)S(1)} %collective-permute-done.4.refs_4_), channel_id=1, source_target_pairs={{0,224},{8,232},{16,240},{24,248},{32,0},{40,8},{48,16},{56,24},{6... | collective-permute-start | bytes 589832 | tf_op jit(solution)/shard_map/ppermute | solution.py:42
  24.1 9.3 %collective-permute-start.12 = (bf16[48,2048]{1,0:T(8,128)(2,1)S(1)}, bf16[48,2048]{1,0:T(8,128)(2,1)S(1)}, u32[]{:S(2)}, u32[]{:S(2)}) collective-permute-start(bf16[48,2048]{1,0:T(8,128)(2,1)S(1)} %collective-permute-done.4.refs_4_), channel_id=1, source_target_pairs={{0,8},{8,0},{16,24},{24,16},{32,40},{40,32},{48,56},{56,48},{64,72... | collective-permute-start | bytes 589832 | tf_op jit(solution)/shard_map/ppermute | solution.py:464
  24.7 10.2 %collective-permute-start.10 = (bf16[48,2048]{1,0:T(8,128)(2,1)S(1)}, bf16[48,2048]{1,0:T(8,128)(2,1)S(1)}, u32[]{:S(2)}, u32[]{:S(2)}) collective-permute-start(bf16[48,2048]{1,0:T(8,128)(2,1)S(1)} %collective-permute-done.1.refs_2_), channel_id=1, source_target_pairs={{0,8},{8,0},{16,24},{24,16},{32,40},{40,32},{48,56},{56,48},{64,72... | collective-permute-start | bytes 589832 | tf_op jit(solution)/shard_map/ppermute | solution.py:464
  24.8 10.2 %collective-permute-start.6 = (bf16[48,2048]{1,0:T(8,128)(2,1)S(1)}, bf16[48,2048]{1,0:T(8,128)(2,1)S(1)}, u32[]{:S(2)}, u32[]{:S(2)}) collective-permute-start(bf16[48,2048]{1,0:T(8,128)(2,1)S(1)} %collective-permute-done.5.above.refs_3_.refs_5_), channel_id=1, source_target_pairs={{0,224},{8,232},{16,240},{24,248},{32,0},{40,8},{48,16},{56,24},{6... | collective-permute-start | bytes 589832 | tf_op jit(solution)/shard_map/ppermute | solution.py:42
  28.1 10.3 %collective-permute-start.3 = (bf16[48,2048]{1,0:T(8,128)(2,1)S(1)}, bf16[48,2048]{1,0:T(8,128)(2,1)S(1)}, u32[]{:S(2)}, u32[]{:S(2)}) collective-permute-start(bf16[48,2048]{1,0:T(8,128)(2,1)S(1)} %collective-permute-done.2.below.refs_1_), channel_id=1, source_target_pairs={{0,32},{8,40},{16,48},{24,56},{32,64},{40,72},{48,80},{56,88},{64,... | collective-permute-start | bytes 589832 | tf_op jit(solution)/shard_map/ppermute | solution.py:42
  28.1 10.2 %collective-permute-start.7 = (bf16[48,2048]{1,0:T(8,128)(2,1)S(1)}, bf16[48,2048]{1,0:T(8,128)(2,1)S(1)}, u32[]{:S(2)}, u32[]{:S(2)}) collective-permute-start(bf16[48,2048]{1,0:T(8,128)(2,1)S(1)} %far.1.refs_4_), channel_id=1, source_target_pairs={{0,64},{8,200},{16,80},{24,216},{32,96},{40,232},{48,112},{56,248}... | collective-permute-start | bytes 589832 | tf_op jit(solution)/shard_map/ppermute | solution.py:450
  44.2 10.2 %collective-permute-start.18 = (bf16[48,3200]{1,0:T(8,128)(2,1)S(1)}, bf16[48,3200]{1,0:T(8,128)(2,1)S(1)}, u32[]{:S(2)}, u32[]{:S(2)}) collective-permute-start(bf16[48,3200]{1,0:T(8,128)(2,1)S(1)} %get-tuple-element.53), channel_id=1, source_target_pairs={{0,1},{1,2},{2,3},{3,0},{4,5},{5,6},{6,7},{7,4},{8,9},{9,10},{10,1... | collective-permute-start | bytes 921608 | tf_op jit(solution)/shard_map/ppermute | solution.py:519
  44.7 11.4 %collective-permute-start.19 = (bf16[48,3200]{1,0:T(8,128)(2,1)S(1)}, bf16[48,3200]{1,0:T(8,128)(2,1)S(1)}, u32[]{:S(2)}, u32[]{:S(2)}) collective-permute-start(bf16[48,3200]{1,0:T(8,128)(2,1)S(1)} %get-tuple-element.54), channel_id=1, source_target_pairs={{0,3},{1,0},{2,1},{3,2},{4,7},{5,4},{6,5},{7,6},{8,11},{9,8},{10,9... | collective-permute-start | bytes 921608 | tf_op jit(solution)/shard_map/ppermute | solution.py:520
  46.3 10.4 %collective-permute-start.20 = (bf16[48,3200]{1,0:T(8,128)(2,1)S(1)}, bf16[48,3200]{1,0:T(8,128)(2,1)S(1)}, u32[]{:S(2)}, u32[]{:S(2)}) collective-permute-start(bf16[48,3200]{1,0:T(8,128)(2,1)S(1)} %get-tuple-element.55), channel_id=1, source_target_pairs={{0,4},{1,5},{2,6},{3,7},{4,0},{5,1},{6,2},{7,3},{8,12},{9,13},{10,... | collective-permute-start | bytes 921608 | tf_op jit(solution)/shard_map/ppermute | solution.py:521
  46.6 14.3 %collective-permute-start.16 = (bf16[48,3200]{1,0:T(8,128)(2,1)S(1)}, bf16[48,3200]{1,0:T(8,128)(2,1)S(1)}, u32[]{:S(2)}, u32[]{:S(2)}) collective-permute-start(bf16[48,3200]{1,0:T(8,128)(2,1)S(1)} %get-tuple-element.51), channel_id=1, source_target_pairs={{0,1},{1,2},{2,3},{3,0},{4,5},{5,6},{6,7},{7,4},{8,9},{9,10},{10,1... | collective-permute-start | bytes 921608 | tf_op jit(solution)/shard_map/ppermute | solution.py:522
  48.3 19.9 %collective-permute-start.17 = (bf16[48,3200]{1,0:T(8,128)(2,1)S(1)}, bf16[48,3200]{1,0:T(8,128)(2,1)S(1)}, u32[]{:S(2)}, u32[]{:S(2)}) collective-permute-start(bf16[48,3200]{1,0:T(8,128)(2,1)S(1)} %get-tuple-element.52), channel_id=1, source_target_pairs={{0,3},{1,0},{2,1},{3,2},{4,7},{5,4},{6,5},{7,6},{8,11},{9,8},{10,9... | collective-permute-start | bytes 921608 | tf_op jit(solution)/shard_map/ppermute | solution.py:522
  57.3 11.0 %collective-permute-start.21 = (bf16[48,3200]{1,0:T(8,128)(2,1)S(1)}, bf16[48,3200]{1,0:T(8,128)(2,1)S(1)}, u32[]{:S(2)}, u32[]{:S(2)}) collective-permute-start(bf16[48,3200]{1,0:T(8,128)(2,1)S(1)} %get-tuple-element.56), channel_id=1, source_target_pairs={{0,4},{1,5},{2,6},{3,7},{4,0},{5,1},{6,2},{7,3},{8,12},{9,13},{10,... | collective-permute-start | bytes 921608 | tf_op jit(solution)/shard_map/ppermute | solution.py:532
  57.7 10.6 %collective-permute-start.22 = (bf16[48,3200]{1,0:T(8,128)(2,1)S(1)}, bf16[48,3200]{1,0:T(8,128)(2,1)S(1)}, u32[]{:S(2)}, u32[]{:S(2)}) collective-permute-start(bf16[48,3200]{1,0:T(8,128)(2,1)S(1)} %get-tuple-element.57), channel_id=1, source_target_pairs={{0,2},{1,3},{2,0},{3,1},{4,6},{5,7},{6,4},{7,5},{8,10},{9,11},{10,... | collective-permute-start | bytes 921608 | tf_op jit(solution)/shard_map/ppermute | solution.py:531
  69.0 9.2 %collective-permute-start.23 = (bf16[48,3200]{1,0:T(8,128)(2,1)S(1)}, bf16[48,3200]{1,0:T(8,128)(2,1)S(1)}, u32[]{:S(2)}, u32[]{:S(2)}) collective-permute-start(bf16[48,3200]{1,0:T(8,128)(2,1)S(1)} %hidden.1.own), channel_id=1, source_target_pairs={{0,4},{1,5},{2,6},{3,7},{4,0},{5,1},{6,2},{7,3},{8,12},{9,13},{10,... | collective-permute-start | bytes 921608 | tf_op jit(solution)/shard_map/ppermute | solution.py:543
  70.9 9.5 %collective-permute-start.25 = (bf16[48,3200]{1,0:T(8,128)(2,1)S(1)}, bf16[48,3200]{1,0:T(8,128)(2,1)S(1)}, u32[]{:S(2)}, u32[]{:S(2)}) collective-permute-start(bf16[48,3200]{1,0:T(8,128)(2,1)S(1)} %hidden.1.own), channel_id=1, source_target_pairs={{0,2},{1,3},{2,0},{3,1},{4,6},{5,7},{6,4},{7,5},{8,10},{9,11},{10,... | collective-permute-start | bytes 921608 | tf_op jit(solution)/shard_map/ppermute | solution.py:542
  78.3 13.4 %collective-permute-start.26 = (bf16[96,3200]{1,0:T(8,128)(2,1)S(1)}, bf16[96,3200]{1,0:T(8,128)(2,1)S(1)}, u32[]{:S(2)}, u32[]{:S(2)}) collective-permute-start(bf16[96,3200]{1,0:T(8,128)(2,1)S(1)} %pad_maximum_fusion), channel_id=1, source_target_pairs={{0,1},{1,2},{2,3},{3,0},{4,5},{5,6},{6,7},{7,4},{8,9},{9,10},{10,1... | collective-permute-start | bytes 1843208 | tf_op jit(solution)/shard_map/ppermute | solution.py:545
  79.7 14.3 %collective-permute-start.24 = (bf16[96,3200]{1,0:T(8,128)(2,1)S(1)}, bf16[96,3200]{1,0:T(8,128)(2,1)S(1)}, u32[]{:S(2)}, u32[]{:S(2)}) collective-permute-start(bf16[96,3200]{1,0:T(8,128)(2,1)S(1)} %pad_maximum_fusion), channel_id=1, source_target_pairs={{0,3},{1,0},{2,1},{3,2},{4,7},{5,4},{6,5},{7,6},{8,11},{9,8},{10,9... | collective-permute-start | bytes 1843208 | tf_op jit(solution)/shard_map/ppermute | solution.py:546
  80.4 8.4 %collective-permute-start.27 = (bf16[48,3200]{1,0:T(8,128)(2,1)S(1)}, bf16[48,3200]{1,0:T(8,128)(2,1)S(1)}, u32[]{:S(2)}, u32[]{:S(2)}) collective-permute-start(bf16[48,3200]{1,0:T(8,128)(2,1)S(1)} %collective-permute-done.25.b2), channel_id=1, source_target_pairs={{0,4},{1,5},{2,6},{3,7},{4,0},{5,1},{6,2},{7,3},{8,12},{9,13},{10,... | collective-permute-start | bytes 921608 | tf_op jit(solution)/shard_map/ppermute | solution.py:547
  99.4 10.8 %collective-permute-start.31 = (bf16[56,1024]{1,0:T(8,128)(2,1)S(1)}, bf16[56,1024]{1,0:T(8,128)(2,1)S(1)}, u32[]{:S(2)}, u32[]{:S(2)}) collective-permute-start(bf16[56,1024]{1,0:T(8,128)(2,1)S(1)} %get-tuple-element.65), channel_id=1, source_target_pairs={{0,32},{8,40},{16,48},{24,56},{32,64},{40,72},{48,80},{56,88},{64,... | collective-permute-start | bytes 344072 | tf_op jit(solution)/shard_map/ppermute | solution.py:42
  106.9 10.4 %collective-permute-start.29 = (bf16[56,1024]{1,0:T(8,128)(2,1)S(1)}, bf16[56,1024]{1,0:T(8,128)(2,1)S(1)}, u32[]{:S(2)}, u32[]{:S(2)}) collective-permute-start(bf16[56,1024]{1,0:T(8,128)(2,1)S(1)} %get-tuple-element.63), channel_id=1, source_target_pairs={{0,32},{8,40},{16,48},{24,56},{32,64},{40,72},{48,80},{56,88},{64,... | collective-permute-start | bytes 344072 | tf_op jit(solution)/shard_map/ppermute | solution.py:42
  107.4 9.9 %collective-permute-start.30 = (bf16[56,1024]{1,0:T(8,128)(2,1)S(1)}, bf16[56,1024]{1,0:T(8,128)(2,1)S(1)}, u32[]{:S(2)}, u32[]{:S(2)}) collective-permute-start(bf16[56,1024]{1,0:T(8,128)(2,1)S(1)} %get-tuple-element.64), channel_id=1, source_target_pairs={{0,224},{8,232},{16,240},{24,248},{32,0},{40,8},{48,16},{56,24},{6... | collective-permute-start | bytes 344072 | tf_op jit(solution)/shard_map/ppermute | solution.py:42
  110.4 8.4 %collective-permute-start.34 = (bf16[56,1024]{1,0:T(8,128)(2,1)S(1)}, bf16[56,1024]{1,0:T(8,128)(2,1)S(1)}, u32[]{:S(2)}, u32[]{:S(2)}) collective-permute-start(bf16[56,1024]{1,0:T(8,128)(2,1)S(1)} %get-tuple-element.68), channel_id=1, source_target_pairs={{0,64},{8,72},{16,80},{24,88},{32,96},{40,104},{48,112},{56,120},{... | collective-permute-start | bytes 344072 | tf_op jit(solution)/shard_map/ppermute | solution.py:42
  110.5 8.3 %collective-permute-start.35 = (bf16[56,1024]{1,0:T(8,128)(2,1)S(1)}, bf16[56,1024]{1,0:T(8,128)(2,1)S(1)}, u32[]{:S(2)}, u32[]{:S(2)}) collective-permute-start(bf16[56,1024]{1,0:T(8,128)(2,1)S(1)} %get-tuple-element.69), channel_id=1, source_target_pairs={{0,192},{8,200},{16,208},{24,216},{32,224},{40,232},{48,240},{56,2... | collective-permute-start | bytes 344072 | tf_op jit(solution)/shard_map/ppermute | solution.py:42
  (25 other events, 165.9 us)

commit v2 on v1

--- a/solution.py
+++ b/solution.py
@@ -122,28 +122,25 @@
     return jnp.where((k == rank) & marked, 1.0, 0.0).astype(bf16), first, last
 
 
-def own_kernel(sel_hbm, tok_hbm, go_hbm, out, row, sel, tok, go, sems):
-    copies = [
-        pltpu.make_async_copy(tok_hbm, tok, sems.at[0]),
-        pltpu.make_async_copy(go_hbm, go, sems.at[1]),
-        pltpu.make_async_copy(sel_hbm, sel, sems.at[2]),
-    ]
+def own_kernel(sel_hbm, tok_hbm, go_hbm, gain_hbm, rw_hbm, out, row, vectors, *held):
+    *held, sems = held
+    sources = (sel_hbm, tok_hbm, go_hbm, gain_hbm, rw_hbm)
+    copies = [pltpu.make_async_copy(sources[n], held[n], sems.at[n]) for n in range(5)]
     for copy in copies:
         copy.start()
-    copies[2].wait()
-    sel_row = sel[...].reshape(1, SEL)
+    copies[0].wait()
+    sel_row = held[0][...].reshape(1, SEL)
     row[...] = sel_row
     pick = pick_of(sel_row)[0]
-    for n, held in enumerate((tok, go)):
-        copies[n].wait()
-        out[:, n * W : n * W + W] = mm(pick, held[...], 0, 0).astype(bf16)
-
-
-def onehot_kernel(sel_row, *refs):
-    sources, (put, spread, vectors), held, sems = refs[:2], refs[2:5], refs[5:7], refs[7]
-    loads = [pltpu.make_async_copy(sources[n], held[n], sems.at[n]) for n in range(2)]
-    for load in loads:
-        load.start()
+    for n in range(2):
+        copies[1 + n].wait()
+        out[:, n * W : n * W + W] = mm(pick, held[1 + n][...], 0, 0).astype(bf16)
+    for n in range(2):
+        copies[3 + n].wait()
+        vectors[n : n + 1, :] = held[3 + n][...]
+
+
+def onehot_kernel(sel_row, put, spread):
     eye = lax.broadcasted_iota(i32, (SEL, SEL), 0) == lax.broadcasted_iota(i32, (SEL, SEL), 1)
     sel_col = jnp.sum(jnp.where(eye, sel_row[...], 0), axis=1, keepdims=True)
 
@@ -152,11 +149,6 @@
         hot = placement(sel_col, i * 128, 128)
         put[:, span(i, 128)] = hot.astype(bf16)
         spread[span(i, 128), :] = hot.T.astype(bf16)
-
-    for load in loads:
-        load.wait()
-    vectors[0:1, :] = held[0][...]
-    vectors[1:2, :] = held[1][...]
 
 
 def stage_kernel(*refs):
@@ -233,9 +225,9 @@
         (to_far, (keep.at[96:144], from_y)),
     ):
 
-        @pl.loop(0, 3 * W // WIDER)
+        @pl.loop(0, 3 * W // W)
         def _(k, out=out, refs=refs):
-            cols = span(k, WIDER)
+            cols = span(k, W)
             total = refs[0][:, cols].astype(f32)
             for ref in refs[1:]:
                 total = total + ref[:, cols].astype(f32)
@@ -420,15 +412,15 @@
     inner = place(summed[2:3, SEL : 2 * SEL])
     held[...] = own
 
-    @pl.loop(0, W // TILE)
+    @pl.loop(0, W // WIDER)
     def _(i):
-        cols = span(i, TILE)
+        cols = span(i, WIDER)
         d_sel = (
             scale * vectors[0:1, cols] * held[:, cols]
             - mine[:, cols].astype(f32) * (scale * scale * inner / D)
             + router_grad * vectors[1:2, cols]
         )
-        spread = jnp.zeros((TOK, TILE), f32)
+        spread = jnp.zeros((TOK, WIDER), f32)
         for piece in heads(d_sel, 3):
             spread += mm(pick, piece.astype(bf16), 1, 0)
         grad_x[:, cols] = (go[:, cols].astype(f32) + spread).astype(bf16)
@@ -468,33 +460,33 @@
     gain = gain.reshape(1, W)
     router_weight = router_weight.reshape(1, W)
     anywhere = pl.BlockSpec(memory_space=pl.ANY)
-    mine, sel_row = pl.pallas_call(
+    mine, sel_row, vectors = pl.pallas_call(
         own_kernel,
         out_shape=(
             jax.ShapeDtypeStruct((CAP, 2 * W), bf16),
             jax.ShapeDtypeStruct((1, SEL), i32),
+            jax.ShapeDtypeStruct((2, W), f32),
         ),
-        in_specs=[anywhere] * 3,
-        out_specs=(VMEM, VMEM),
+        in_specs=[anywhere] * 5,
+        out_specs=(VMEM,) * 3,
         scratch_shapes=[pltpu.VMEM((SEL,), i32)]
         + [pltpu.VMEM((TOK, W), bf16)] * 2
-        + [pltpu.SemaphoreType.DMA((3,))],
+        + [pltpu.VMEM((1, W), f32)] * 2
+        + [pltpu.SemaphoreType.DMA((5,))],
         compiler_params=params(60),
         name="own",
-    )(selected, tokens, grad_out)
-    put, spread, vectors = pl.pallas_call(
+    )(selected, tokens, grad_out, gain, router_weight)
+    put, spread = pl.pallas_call(
         onehot_kernel,
         out_shape=(
             jax.ShapeDtypeStruct((SEL, 2 * SEL), bf16),
             jax.ShapeDtypeStruct((2 * SEL, SEL), bf16),
-            jax.ShapeDtypeStruct((2, W), f32),
         ),
-        in_specs=[VMEM] + [anywhere] * 2,
-        out_specs=(VMEM,) * 3,
-        scratch_shapes=[pltpu.VMEM((1, W), f32)] * 2 + [pltpu.SemaphoreType.DMA((2,))],
+        in_specs=[VMEM],
+        out_specs=(VMEM,) * 2,
         compiler_params=params(16),
         name="onehot",
-    )(sel_row, gain, router_weight)
+    )(sel_row)
     pair = jnp.concatenate([mine, lax.ppermute(mine, "wide", YLO)], axis=0)
     parts, weights = gather(pair, put, w_gate, w_up, w_down)
 

time: 127 us -> 126 us (level)
  waiting for transfers between devices: 49.6 us -> 51.7 us
  starting transfers between devices: 43.5 us -> 41.8 us
  local copies, waits for them, and re-layouts: 8.02 us -> 6.65 us
    ppermute x8, starting transfers between devices: 3.19 us -> 1.63 us  [gather(): lax.ppermute(piece, 'wide', CORE)]
    unnamed x32 -> x30, local copies, waits for them, and re-layouts: 7.99 us -> 6.62 us
  transfers between devices with their start and end apart: 37 -> 37, of which waited for: 17 -> 21; matrix products, arithmetic and copies ran while one was open for 8% -> 8% of each run, Pallas kernels for 2% -> 2%
where the time goes in v2:
time: 126 us; the launch traced here: 124 us
  waiting for transfers between devices  51.7 us (41%)
  starting transfers between devices  41.8 us (33%)
  Pallas kernels  14.2 us (11%)
  matrix products  8.06 us (6%)
  local copies, waits for them, and re-layouts  6.65 us (5%)
    ppermute x12, starting transfers between devices, along(): lax.ppermute(value, 'wide', wide_pairs(lambda z, y, c: (z + 8 + step, y,...  24.1 us
    dot_general x3, matrix products, mm(): lax.dot_general(a, b, (((ca,), (cb,)), ((), ())), preferred_element_type=...  8.06 us
    ppermute x12, waiting for transfers between devices, along(): lax.ppermute(value, 'wide', wide_pairs(lambda z, y, c: (z + 8 + step, y,...  7.36 us
    ppermute x1, waiting for transfers between devices, local(): lax.ppermute(near[1], 'narrow', XDOWN)  7.19 us
    unnamed x30, local copies, waits for them, and re-layouts  6.62 us
    ppermute x1, waiting for transfers between devices, local(): b6 = lax.ppermute(b2, 'narrow', YHI)  6.46 us
    ppermute x1, waiting for transfers between devices, local(): b4 = lax.ppermute(own, 'narrow', YHI)  6.1 us
    ppermute x1, waiting for transfers between devices, local(): from_below = lax.ppermute(to_up, 'narrow', XUP)  5.73 us
  transfers between devices with their start and end apart: 37, of which 21 were waited for; matrix products, arithmetic and copies ran while one was open for 8% of the time, Pallas kernels for 2%

profile of v2, /device:TPU:22, one launch (start us, length us, event | category | flops | bytes accessed | tf_op | source)
XLA Modules:
  0.0 123.6 jit_solution(10063844139940968751)
XLA Ops:
  0.6 2.0 %own.1 = (bf16[24,2048]{1,0:T(8,128)(2,1)}, s32[1,384]{1,0:T(1,128)}, f32[2,1024]{1,0:T(2,128)}) custom-call(s32[384]{0:T(512)} %sel_hbm.1, bf16[96,1024]{1,0:T(8,128)(2,1)} %tok_hbm.1, bf16[96,1024]{1,0:T(8,128)(2,1)} %go.1, f32[1,1024]{1,0:T(1,128)} %bitcast.5, f32[1,1024]{1,0:T(1,128)} %bitcast.4), custom_call_target="tpu_custom_call" | custom-call | tf_op jit(solution)/shard_map/own/pallas_call | solution.py:463
  4.9 2.6 %collective-permute-done = bf16[24,2048]{1,0:T(8,128)(2,1)S(1)} collective-permute-done((bf16[24,2048]{1,0:T(8,128)(2,1)}, bf16[24,2048]{1,0:T(8,128)(2,1)S(1)}, u32[]{:S(2)}, u32[]{:S(2)}) %collective-permute-start) | collective-permute-done | bytes 98336 | tf_op jit(solution)/shard_map/ppermute | solution.py:490
  7.6 5.9 %collective-permute-start.4 = (bf16[48,2048]{1,0:T(8,128)(2,1)S(1)}, bf16[48,2048]{1,0:T(8,128)(2,1)S(1)}, u32[]{:S(2)}, u32[]{:S(2)}) collective-permute-start(bf16[48,2048]{1,0:T(8,128)(2,1)S(1)} %constant_dynamic-update-slice_fusion.refs_3_), channel_id=1, source_target_pairs={{0,224},{8,232},{16,240},{24,248},{32,0},{40,8},{48,16},{56,24},{6... | collective-permute-start | bytes 589832 | tf_op jit(solution)/shard_map/ppermute | solution.py:42
  13.5 3.2 %collective-permute-done.4.refs_4_ = bf16[48,2048]{1,0:T(8,128)(2,1)S(1)} collective-permute-done((bf16[48,2048]{1,0:T(8,128)(2,1)S(1)}, bf16[48,2048]{1,0:T(8,128)(2,1)S(1)}, u32[]{:S(2)}, u32[]{:S(2)}) %collective-permute-start.4) | collective-permute-done | bytes 196640 | tf_op jit(solution)/shard_map/ppermute | solution.py:42
  16.7 3.7 %collective-permute-start.5 = (bf16[48,2048]{1,0:T(8,128)(2,1)S(1)}, bf16[48,2048]{1,0:T(8,128)(2,1)S(1)}, u32[]{:S(2)}, u32[]{:S(2)}) collective-permute-start(bf16[48,2048]{1,0:T(8,128)(2,1)S(1)} %collective-permute-done.4.refs_4_), channel_id=1, source_target_pairs={{0,224},{8,232},{16,240},{24,248},{32,0},{40,8},{48,16},{56,24},{6... | collective-permute-start | bytes 589832 | tf_op jit(solution)/shard_map/ppermute | solution.py:42
  23.6 3.7 %collective-permute-start.6 = (bf16[48,2048]{1,0:T(8,128)(2,1)S(1)}, bf16[48,2048]{1,0:T(8,128)(2,1)S(1)}, u32[]{:S(2)}, u32[]{:S(2)}) collective-permute-start(bf16[48,2048]{1,0:T(8,128)(2,1)S(1)} %collective-permute-done.5.above.refs_3_.refs_5_), channel_id=1, source_target_pairs={{0,224},{8,232},{16,240},{24,248},{32,0},{40,8},{48,16},{56,24},{6... | collective-permute-start | bytes 589832 | tf_op jit(solution)/shard_map/ppermute | solution.py:42
  34.5 2.3 %collective-permute-done.3.refs_0_ = bf16[48,2048]{1,0:T(8,128)(2,1)S(1)} collective-permute-done((bf16[48,2048]{1,0:T(8,128)(2,1)S(1)}, bf16[48,2048]{1,0:T(8,128)(2,1)S(1)}, u32[]{:S(2)}, u32[]{:S(2)}) %collective-permute-start.3) | collective-permute-done | bytes 196640 | tf_op jit(solution)/shard_map/ppermute | solution.py:42
  39.2 4.1 %forward.1 = (bf16[384,1024]{1,0:T(8,128)(2,1)S(1)}, bf16[384,1024]{1,0:T(8,128)(2,1)S(1)}, bf16[144,3200]{1,0:T(8,128)(2,1)S(1)}, bf16[48,3200]{1,0:T(8,128)(2,...) custom-call(bf16[48,2048]{1,0:T(8,128)(2,1)S(1)} %collective-permute, ...), custom_call_target="tpu_custom_call" | custom-call | flops 3600000000 | bytes 16000000 | tf_op jit(solution)/shard_map/forward/pallas_call | solution.py:495
  47.7 5.7 %collective-permute-done.18.from_below = bf16[48,3200]{1,0:T(8,128)(2,1)S(1)} collective-permute-done((bf16[48,3200]{1,0:T(8,128)(2,1)S(1)}, bf16[48,3200]{1,0:T(8,128)(2,1)S(1)}, u32[]{:S(2)}, u32[]{:S(2)}) %collective-permute-start.18) | collective-permute-done | bytes 307232 | tf_op jit(solution)/shard_map/ppermute | solution.py:511
  58.1 2.0 %collective-permute-done.16.near_below = bf16[48,3200]{1,0:T(8,128)(2,1)S(1)} collective-permute-done((bf16[48,3200]{1,0:T(8,128)(2,1)S(1)}, bf16[48,3200]{1,0:T(8,128)(2,1)S(1)}, u32[]{:S(2)}, u32[]{:S(2)}) %collective-permute-start.16) | collective-permute-done | bytes 307232 | tf_op jit(solution)/shard_map/ppermute | solution.py:514
  60.1 7.2 %collective-permute-done.17.near_above = bf16[48,3200]{1,0:T(8,128)(2,1)S(1)} collective-permute-done((bf16[48,3200]{1,0:T(8,128)(2,1)S(1)}, bf16[48,3200]{1,0:T(8,128)(2,1)S(1)}, u32[]{:S(2)}, u32[]{:S(2)}) %collective-permute-start.17) | collective-permute-done | bytes 307232 | tf_op jit(solution)/shard_map/ppermute | solution.py:514
  71.2 6.1 %collective-permute-done.23.b4 = bf16[48,3200]{1,0:T(8,128)(2,1)S(1)} collective-permute-done((bf16[48,3200]{1,0:T(8,128)(2,1)S(1)}, bf16[48,3200]{1,0:T(8,128)(2,1)S(1)}, u32[]{:S(2)}, u32[]{:S(2)}) %collective-permute-start.23) | collective-permute-done | bytes 307232 | tf_op jit(solution)/shard_map/ppermute | solution.py:535
  79.4 1.9 %collective-permute-start.27 = (bf16[48,3200]{1,0:T(8,128)(2,1)S(1)}, bf16[48,3200]{1,0:T(8,128)(2,1)S(1)}, u32[]{:S(2)}, u32[]{:S(2)}) collective-permute-start(bf16[48,3200]{1,0:T(8,128)(2,1)S(1)} %collective-permute-done.25.b2), channel_id=1, source_target_pairs={{0,4},{1,5},{2,6},{3,7},{4,0},{5,1},{6,2},{7,3},{8,12},{9,13},{10,... | collective-permute-start | bytes 921608 | tf_op jit(solution)/shard_map/ppermute | solution.py:539
  81.3 6.5 %collective-permute-done.27.b6 = bf16[48,3200]{1,0:T(8,128)(2,1)S(1)} collective-permute-done((bf16[48,3200]{1,0:T(8,128)(2,1)S(1)}, bf16[48,3200]{1,0:T(8,128)(2,1)S(1)}, u32[]{:S(2)}, u32[]{:S(2)}) %collective-permute-start.27) | collective-permute-done | bytes 307232 | tf_op jit(solution)/shard_map/ppermute | solution.py:539
  87.8 2.9 %collective-permute-done.26.below = bf16[96,3200]{1,0:T(8,128)(2,1)S(1)} collective-permute-done((bf16[96,3200]{1,0:T(8,128)(2,1)S(1)}, bf16[96,3200]{1,0:T(8,128)(2,1)S(1)}, u32[]{:S(2)}, u32[]{:S(2)}) %collective-permute-start.26) | collective-permute-done | bytes 614432 | tf_op jit(solution)/shard_map/ppermute | solution.py:537
  90.7 2.4 %collective-permute-done.24.above = bf16[96,3200]{1,0:T(8,128)(2,1)S(1)} collective-permute-done((bf16[96,3200]{1,0:T(8,128)(2,1)S(1)}, bf16[96,3200]{1,0:T(8,128)(2,1)S(1)}, u32[]{:S(2)}, u32[]{:S(2)}) %collective-permute-start.24) | collective-permute-done | bytes 614432 | tf_op jit(solution)/shard_map/ppermute | solution.py:538
  93.1 2.8 %normed.1 = (bf16[392,1024]{1,0:T(8,128)(2,1)S(1)}, bf16[384,1024]{1,0:T(8,128)(2,1)S(1)}, f32[8,1024]{1,0:T(8,128)S(1)}) custom-call(bf16[768,384]{1,0:T(8,128)(2,1)S(1)} %get-tuple-element.42.spread, bf16[48,3200]{1,0:T(8,128)(2,1)S(1)} %hidden.1.own, bf16[96,3200]{1,0:T(8,128)(2,1)S(1)} %collective-permute-done.24.above, ...), custom_call_target="tpu_custom_call" | custom-call | flops 2400000000 | bytes 9000000 | tf_op jit(solution)/shard_map/normed/pallas_call | solution.py:541
  96.6 1.8 %collective-permute-done.28.theirs.up2_other.down2_other.stay_other = bf16[392,1024]{1,0:T(8,128)(2,1)S(1)} collective-permute-done((bf16[392,1024]{1,0:T(8,128)(2,1)S(1)}, bf16[392,1024]{1,0:T(8,128)(2,1)S(1)}, u32[]{:S(2)}, u32[]{:S(2)}) %collective-permute-start.28) | collective-permute-done | bytes 802848 | tf_op jit(solution)/shard_map/ppermute | solution.py:564
  98.5 2.8 %collective-permute-start.31 = (bf16[56,1024]{1,0:T(8,128)(2,1)S(1)}, bf16[56,1024]{1,0:T(8,128)(2,1)S(1)}, u32[]{:S(2)}, u32[]{:S(2)}) collective-permute-start(bf16[56,1024]{1,0:T(8,128)(2,1)S(1)} %get-tuple-element.65), channel_id=1, source_target_pairs={{0,32},{8,40},{16,48},{24,56},{32,64},{40,72},{48,80},{56,88},{64,... | collective-permute-start | bytes 344072 | tf_op jit(solution)/shard_map/ppermute | solution.py:42
  102.9 2.7 %convolution_convert_fusion.1 = bf16[1024,1024]{1,0:T(8,128)(2,1)} fusion(bf16[384,3200]{1,0:T(8,128)(2,1)S(1)} %slice_dynamic-update-slice_fusion, bf16[384,1024]{1,0:T(8,128)(2,1)S(1)} %get-tuple-element.58.sel, f32[1024]{0:T(1024)S(1)} %copy-done.10, f32[384]{0:T(512)S(1)} %get-tuple-element.77), kind=kOutput, calls=%fused_computation.1 | convolution fusion | flops 807927808 | bytes 3676160 | tf_op jit(solution)/shard_map/dot_general | solution.py:78
  106.0 2.8 %collective-permute-start.30 = (bf16[56,1024]{1,0:T(8,128)(2,1)S(1)}, bf16[56,1024]{1,0:T(8,128)(2,1)S(1)}, u32[]{:S(2)}, u32[]{:S(2)}) collective-permute-start(bf16[56,1024]{1,0:T(8,128)(2,1)S(1)} %get-tuple-element.64), channel_id=1, source_target_pairs={{0,224},{8,232},{16,240},{24,248},{32,0},{40,8},{48,16},{56,24},{6... | collective-permute-start | bytes 344072 | tf_op jit(solution)/shard_map/ppermute | solution.py:42
  110.2 4.1 %collective-permute-start.35 = (bf16[56,1024]{1,0:T(8,128)(2,1)S(1)}, bf16[56,1024]{1,0:T(8,128)(2,1)S(1)}, u32[]{:S(2)}, u32[]{:S(2)}) collective-permute-start(bf16[56,1024]{1,0:T(8,128)(2,1)S(1)} %get-tuple-element.69), channel_id=1, source_target_pairs={{0,192},{8,200},{16,208},{24,216},{32,224},{40,232},{48,240},{56,2... | collective-permute-start | bytes 344072 | tf_op jit(solution)/shard_map/ppermute | solution.py:42
  114.3 2.7 %convolution_convert_fusion.2 = bf16[1024,1024]{1,0:T(8,128)(2,1)} fusion(bf16[384,3200]{1,0:T(8,128)(2,1)S(1)} %slice_dynamic-update-slice_fusion, bf16[384,1024]{1,0:T(8,128)(2,1)S(1)} %get-tuple-element.58.sel, f32[1024]{0:T(1024)S(1)} %copy-done.10, f32[384]{0:T(512)S(1)} %get-tuple-element.77), kind=kOutput, calls=%fused_computation.2 | convolution fusion | flops 807927808 | bytes 3676160 | tf_op jit(solution)/shard_map/dot_general | solution.py:78
  118.0 2.7 %convolution_convert_fusion = bf16[1024,1024]{1,0:T(8,128)(2,1)} fusion(bf16[384,1024]{1,0:T(8,128)(2,1)S(1)} %get-tuple-element.73, bf16[384,3200]{1,0:T(8,128)(2,1)S(1)} %slice_dynamic-update-slice_fusion, f32[384]{0:T(512)S(1)} %get-tuple-element.76), kind=kOutput, calls=%fused_computation | convolution fusion | flops 807534592 | bytes 3672064 | tf_op jit(solution)/shard_map/dot_general | solution.py:78
  (100 shorter events, 38.2 us)
Async XLA Ops:
  7.6 9.1 %collective-permute-start.4 = (bf16[48,2048]{1,0:T(8,128)(2,1)S(1)}, bf16[48,2048]{1,0:T(8,128)(2,1)S(1)}, u32[]{:S(2)}, u32[]{:S(2)}) collective-permute-start(bf16[48,2048]{1,0:T(8,128)(2,1)S(1)} %constant_dynamic-update-slice_fusion.refs_3_), channel_id=1, source_target_pairs={{0,224},{8,232},{16,240},{24,248},{32,0},{40,8},{48,16},{56,24},{6... | collective-permute-start | bytes 589832 | tf_op jit(solution)/shard_map/ppermute | solution.py:42
  22.7 10.0 %collective-permute-start.12 = (bf16[48,2048]{1,0:T(8,128)(2,1)S(1)}, bf16[48,2048]{1,0:T(8,128)(2,1)S(1)}, u32[]{:S(2)}, u32[]{:S(2)}) collective-permute-start(bf16[48,2048]{1,0:T(8,128)(2,1)S(1)} %collective-permute-done.4.refs_4_), channel_id=1, source_target_pairs={{0,8},{8,0},{16,24},{24,16},{32,40},{40,32},{48,56},{56,48},{64,72... | collective-permute-start | bytes 589832 | tf_op jit(solution)/shard_map/ppermute | solution.py:456
  23.3 10.2 %collective-permute-start.10 = (bf16[48,2048]{1,0:T(8,128)(2,1)S(1)}, bf16[48,2048]{1,0:T(8,128)(2,1)S(1)}, u32[]{:S(2)}, u32[]{:S(2)}) collective-permute-start(bf16[48,2048]{1,0:T(8,128)(2,1)S(1)} %collective-permute-done.1.refs_2_), channel_id=1, source_target_pairs={{0,8},{8,0},{16,24},{24,16},{32,40},{40,32},{48,56},{56,48},{64,72... | collective-permute-start | bytes 589832 | tf_op jit(solution)/shard_map/ppermute | solution.py:456
  23.6 11.0 %collective-permute-start.6 = (bf16[48,2048]{1,0:T(8,128)(2,1)S(1)}, bf16[48,2048]{1,0:T(8,128)(2,1)S(1)}, u32[]{:S(2)}, u32[]{:S(2)}) collective-permute-start(bf16[48,2048]{1,0:T(8,128)(2,1)S(1)} %collective-permute-done.5.above.refs_3_.refs_5_), channel_id=1, source_target_pairs={{0,224},{8,232},{16,240},{24,248},{32,0},{40,8},{48,16},{56,24},{6... | collective-permute-start | bytes 589832 | tf_op jit(solution)/shard_map/ppermute | solution.py:42
  27.3 9.6 %collective-permute-start.3 = (bf16[48,2048]{1,0:T(8,128)(2,1)S(1)}, bf16[48,2048]{1,0:T(8,128)(2,1)S(1)}, u32[]{:S(2)}, u32[]{:S(2)}) collective-permute-start(bf16[48,2048]{1,0:T(8,128)(2,1)S(1)} %collective-permute-done.2.below.refs_1_), channel_id=1, source_target_pairs={{0,32},{8,40},{16,48},{24,56},{32,64},{40,72},{48,80},{56,88},{64,... | collective-permute-start | bytes 589832 | tf_op jit(solution)/shard_map/ppermute | solution.py:42
  27.3 10.4 %collective-permute-start.7 = (bf16[48,2048]{1,0:T(8,128)(2,1)S(1)}, bf16[48,2048]{1,0:T(8,128)(2,1)S(1)}, u32[]{:S(2)}, u32[]{:S(2)}) collective-permute-start(bf16[48,2048]{1,0:T(8,128)(2,1)S(1)} %far.1.refs_4_), channel_id=1, source_target_pairs={{0,64},{8,200},{16,80},{24,216},{32,96},{40,232},{48,112},{56,248}... | collective-permute-start | bytes 589832 | tf_op jit(solution)/shard_map/ppermute | solution.py:442
  43.3 10.2 %collective-permute-start.18 = (bf16[48,3200]{1,0:T(8,128)(2,1)S(1)}, bf16[48,3200]{1,0:T(8,128)(2,1)S(1)}, u32[]{:S(2)}, u32[]{:S(2)}) collective-permute-start(bf16[48,3200]{1,0:T(8,128)(2,1)S(1)} %get-tuple-element.53), channel_id=1, source_target_pairs={{0,1},{1,2},{2,3},{3,0},{4,5},{5,6},{6,7},{7,4},{8,9},{9,10},{10,1... | collective-permute-start | bytes 921608 | tf_op jit(solution)/shard_map/ppermute | solution.py:511
  43.8 11.4 %collective-permute-start.19 = (bf16[48,3200]{1,0:T(8,128)(2,1)S(1)}, bf16[48,3200]{1,0:T(8,128)(2,1)S(1)}, u32[]{:S(2)}, u32[]{:S(2)}) collective-permute-start(bf16[48,3200]{1,0:T(8,128)(2,1)S(1)} %get-tuple-element.54), channel_id=1, source_target_pairs={{0,3},{1,0},{2,1},{3,2},{4,7},{5,4},{6,5},{7,6},{8,11},{9,8},{10,9... | collective-permute-start | bytes 921608 | tf_op jit(solution)/shard_map/ppermute | solution.py:512
  45.4 10.3 %collective-permute-start.20 = (bf16[48,3200]{1,0:T(8,128)(2,1)S(1)}, bf16[48,3200]{1,0:T(8,128)(2,1)S(1)}, u32[]{:S(2)}, u32[]{:S(2)}) collective-permute-start(bf16[48,3200]{1,0:T(8,128)(2,1)S(1)} %get-tuple-element.55), channel_id=1, source_target_pairs={{0,4},{1,5},{2,6},{3,7},{4,0},{5,1},{6,2},{7,3},{8,12},{9,13},{10,... | collective-permute-start | bytes 921608 | tf_op jit(solution)/shard_map/ppermute | solution.py:513
  45.7 14.3 %collective-permute-start.16 = (bf16[48,3200]{1,0:T(8,128)(2,1)S(1)}, bf16[48,3200]{1,0:T(8,128)(2,1)S(1)}, u32[]{:S(2)}, u32[]{:S(2)}) collective-permute-start(bf16[48,3200]{1,0:T(8,128)(2,1)S(1)} %get-tuple-element.51), channel_id=1, source_target_pairs={{0,1},{1,2},{2,3},{3,0},{4,5},{5,6},{6,7},{7,4},{8,9},{9,10},{10,1... | collective-permute-start | bytes 921608 | tf_op jit(solution)/shard_map/ppermute | solution.py:514
  47.4 19.8 %collective-permute-start.17 = (bf16[48,3200]{1,0:T(8,128)(2,1)S(1)}, bf16[48,3200]{1,0:T(8,128)(2,1)S(1)}, u32[]{:S(2)}, u32[]{:S(2)}) collective-permute-start(bf16[48,3200]{1,0:T(8,128)(2,1)S(1)} %get-tuple-element.52), channel_id=1, source_target_pairs={{0,3},{1,0},{2,1},{3,2},{4,7},{5,4},{6,5},{7,6},{8,11},{9,8},{10,9... | collective-permute-start | bytes 921608 | tf_op jit(solution)/shard_map/ppermute | solution.py:514
  56.2 11.0 %collective-permute-start.21 = (bf16[48,3200]{1,0:T(8,128)(2,1)S(1)}, bf16[48,3200]{1,0:T(8,128)(2,1)S(1)}, u32[]{:S(2)}, u32[]{:S(2)}) collective-permute-start(bf16[48,3200]{1,0:T(8,128)(2,1)S(1)} %get-tuple-element.56), channel_id=1, source_target_pairs={{0,4},{1,5},{2,6},{3,7},{4,0},{5,1},{6,2},{7,3},{8,12},{9,13},{10,... | collective-permute-start | bytes 921608 | tf_op jit(solution)/shard_map/ppermute | solution.py:524
  56.6 10.6 %collective-permute-start.22 = (bf16[48,3200]{1,0:T(8,128)(2,1)S(1)}, bf16[48,3200]{1,0:T(8,128)(2,1)S(1)}, u32[]{:S(2)}, u32[]{:S(2)}) collective-permute-start(bf16[48,3200]{1,0:T(8,128)(2,1)S(1)} %get-tuple-element.57), channel_id=1, source_target_pairs={{0,2},{1,3},{2,0},{3,1},{4,6},{5,7},{6,4},{7,5},{8,10},{9,11},{10,... | collective-permute-start | bytes 921608 | tf_op jit(solution)/shard_map/ppermute | solution.py:523
  68.0 9.2 %collective-permute-start.23 = (bf16[48,3200]{1,0:T(8,128)(2,1)S(1)}, bf16[48,3200]{1,0:T(8,128)(2,1)S(1)}, u32[]{:S(2)}, u32[]{:S(2)}) collective-permute-start(bf16[48,3200]{1,0:T(8,128)(2,1)S(1)} %hidden.1.own), channel_id=1, source_target_pairs={{0,4},{1,5},{2,6},{3,7},{4,0},{5,1},{6,2},{7,3},{8,12},{9,13},{10,... | collective-permute-start | bytes 921608 | tf_op jit(solution)/shard_map/ppermute | solution.py:535
  69.8 9.7 %collective-permute-start.25 = (bf16[48,3200]{1,0:T(8,128)(2,1)S(1)}, bf16[48,3200]{1,0:T(8,128)(2,1)S(1)}, u32[]{:S(2)}, u32[]{:S(2)}) collective-permute-start(bf16[48,3200]{1,0:T(8,128)(2,1)S(1)} %hidden.1.own), channel_id=1, source_target_pairs={{0,2},{1,3},{2,0},{3,1},{4,6},{5,7},{6,4},{7,5},{8,10},{9,11},{10,... | collective-permute-start | bytes 921608 | tf_op jit(solution)/shard_map/ppermute | solution.py:534
  77.3 13.4 %collective-permute-start.26 = (bf16[96,3200]{1,0:T(8,128)(2,1)S(1)}, bf16[96,3200]{1,0:T(8,128)(2,1)S(1)}, u32[]{:S(2)}, u32[]{:S(2)}) collective-permute-start(bf16[96,3200]{1,0:T(8,128)(2,1)S(1)} %pad_maximum_fusion), channel_id=1, source_target_pairs={{0,1},{1,2},{2,3},{3,0},{4,5},{5,6},{6,7},{7,4},{8,9},{9,10},{10,1... | collective-permute-start | bytes 1843208 | tf_op jit(solution)/shard_map/ppermute | solution.py:537
  78.8 14.3 %collective-permute-start.24 = (bf16[96,3200]{1,0:T(8,128)(2,1)S(1)}, bf16[96,3200]{1,0:T(8,128)(2,1)S(1)}, u32[]{:S(2)}, u32[]{:S(2)}) collective-permute-start(bf16[96,3200]{1,0:T(8,128)(2,1)S(1)} %pad_maximum_fusion), channel_id=1, source_target_pairs={{0,3},{1,0},{2,1},{3,2},{4,7},{5,4},{6,5},{7,6},{8,11},{9,8},{10,9... | collective-permute-start | bytes 1843208 | tf_op jit(solution)/shard_map/ppermute | solution.py:538
  79.4 8.4 %collective-permute-start.27 = (bf16[48,3200]{1,0:T(8,128)(2,1)S(1)}, bf16[48,3200]{1,0:T(8,128)(2,1)S(1)}, u32[]{:S(2)}, u32[]{:S(2)}) collective-permute-start(bf16[48,3200]{1,0:T(8,128)(2,1)S(1)} %collective-permute-done.25.b2), channel_id=1, source_target_pairs={{0,4},{1,5},{2,6},{3,7},{4,0},{5,1},{6,2},{7,3},{8,12},{9,13},{10,... | collective-permute-start | bytes 921608 | tf_op jit(solution)/shard_map/ppermute | solution.py:539
  98.5 10.3 %collective-permute-start.31 = (bf16[56,1024]{1,0:T(8,128)(2,1)S(1)}, bf16[56,1024]{1,0:T(8,128)(2,1)S(1)}, u32[]{:S(2)}, u32[]{:S(2)}) collective-permute-start(bf16[56,1024]{1,0:T(8,128)(2,1)S(1)} %get-tuple-element.65), channel_id=1, source_target_pairs={{0,32},{8,40},{16,48},{24,56},{32,64},{40,72},{48,80},{56,88},{64,... | collective-permute-start | bytes 344072 | tf_op jit(solution)/shard_map/ppermute | solution.py:42
  101.8 8.1 %collective-permute-start.33 = (bf16[56,1024]{1,0:T(8,128)(2,1)S(1)}, bf16[56,1024]{1,0:T(8,128)(2,1)S(1)}, u32[]{:S(2)}, u32[]{:S(2)}) collective-permute-start(bf16[56,1024]{1,0:T(8,128)(2,1)S(1)} %get-tuple-element.67), channel_id=1, source_target_pairs={{0,64},{8,200},{16,80},{24,216},{32,96},{40,232},{48,112},{56,248}... | collective-permute-start | bytes 344072 | tf_op jit(solution)/shard_map/ppermute | solution.py:574
  105.6 11.4 %collective-permute-start.29 = (bf16[56,1024]{1,0:T(8,128)(2,1)S(1)}, bf16[56,1024]{1,0:T(8,128)(2,1)S(1)}, u32[]{:S(2)}, u32[]{:S(2)}) collective-permute-start(bf16[56,1024]{1,0:T(8,128)(2,1)S(1)} %get-tuple-element.63), channel_id=1, source_target_pairs={{0,32},{8,40},{16,48},{24,56},{32,64},{40,72},{48,80},{56,88},{64,... | collective-permute-start | bytes 344072 | tf_op jit(solution)/shard_map/ppermute | solution.py:42
  106.0 11.0 %collective-permute-start.30 = (bf16[56,1024]{1,0:T(8,128)(2,1)S(1)}, bf16[56,1024]{1,0:T(8,128)(2,1)S(1)}, u32[]{:S(2)}, u32[]{:S(2)}) collective-permute-start(bf16[56,1024]{1,0:T(8,128)(2,1)S(1)} %get-tuple-element.64), channel_id=1, source_target_pairs={{0,224},{8,232},{16,240},{24,248},{32,0},{40,8},{48,16},{56,24},{6... | collective-permute-start | bytes 344072 | tf_op jit(solution)/shard_map/ppermute | solution.py:42
  110.1 7.7 %collective-permute-start.34 = (bf16[56,1024]{1,0:T(8,128)(2,1)S(1)}, bf16[56,1024]{1,0:T(8,128)(2,1)S(1)}, u32[]{:S(2)}, u32[]{:S(2)}) collective-permute-start(bf16[56,1024]{1,0:T(8,128)(2,1)S(1)} %get-tuple-element.68), channel_id=1, source_target_pairs={{0,64},{8,72},{16,80},{24,88},{32,96},{40,104},{48,112},{56,120},{... | collective-permute-start | bytes 344072 | tf_op jit(solution)/shard_map/ppermute | solution.py:42
  110.2 7.6 %collective-permute-start.35 = (bf16[56,1024]{1,0:T(8,128)(2,1)S(1)}, bf16[56,1024]{1,0:T(8,128)(2,1)S(1)}, u32[]{:S(2)}, u32[]{:S(2)}) collective-permute-start(bf16[56,1024]{1,0:T(8,128)(2,1)S(1)} %get-tuple-element.69), channel_id=1, source_target_pairs={{0,192},{8,200},{16,208},{24,216},{32,224},{40,232},{48,240},{56,2... | collective-permute-start | bytes 344072 | tf_op jit(solution)/shard_map/ppermute | solution.py:42
  (24 other events, 173.2 us)
